TPU v7x, 32 devices: a whole 2x2x4 slice. The times are simulated.
32 devices in a mesh: range: 16 (over z, y, core), pulse: 2 (over x).
Axes of the slice: x: 2, y: 2, z: 4, core: 2. Of those that a mesh axis runs over, the one named last changes fastest.
Arguments:
- echoes: float32 [2, 64, 2, 16384], P(None, None, 'pulse', 'range'), may hold values from -6 to 6
- steer_blocks: float32 [32, 2, 32, 8], P('pulse'), may hold values from -0.75 to 0.75
- plan: int32 [8, 4], replicated, may hold values from 0 to 7, as said below
- filter_taps: float32 [2, 1024], replicated, may hold values from -0.125 to 0.125
Outputs:
- compressed: float32 [2, 256, 2, 16384], P(None, 'pulse', None, 'range')
Inputs may be any that keep to these rules, and one draw needn't show every extreme that they name: `plan`: each row names 4 different subarray blocks; rows 2m and 2m + 1 together name every subarray block once.
All inputs are finite; a program needn't handle non-finite values.
Results may differ from a plain program's by a relative error of at most 0.0001.
Values sent between devices are 32-bit elements; how exact they have to be, the bound alone decides.
No kernel may reach another device: no remote copies, remote signals or barrier semaphores. Data moves between devices by JAX's collectives and lax.ppermute only.
A program may use at most 128 MiB of HBM per device.

v0:
```python
import functools

import jax
import jax.numpy as jnp
from jax import lax
from jax.experimental import pallas as pl
from jax.experimental.pallas import tpu as pltpu
from jax.sharding import PartitionSpec as P

TILE = 128
f32 = jnp.float32
bf16 = jnp.bfloat16
VMEM = pl.BlockSpec(memory_space=pltpu.VMEM)
SMEM = pl.BlockSpec(memory_space=pltpu.SMEM)


def dot(left, right):
    return jnp.dot(left, right, preferred_element_type=f32)


def split(value):
    high = value.astype(bf16)
    return high, (value - high.astype(f32)).astype(bf16)


def shifted(value, axis, steps):
    count = lax.axis_size(axis)
    return lax.ppermute(value, axis, [(i, (i + steps) % count) for i in range(count)])


def from_odd(value):
    count = lax.axis_size("range")
    target = {i: (i + 1) % count for i in range(count)}
    source, goal = count - 1, count - 5
    while goal > 0:
        target[source] = goal
        source, goal = goal - 1, goal - 4
    target[source] = 0
    return lax.ppermute(value, "range", list(target.items()))


def from_even(value):
    count = lax.axis_size("range")
    return lax.ppermute(value, "range", [(i, i ^ 1) for i in range(count)])


def make_tables(taps_ref, high_ref, low_ref):
    span = taps_ref.shape[1] // TILE
    row = lax.broadcasted_iota(jnp.int32, (TILE, TILE), 0)
    lane = lax.broadcasted_iota(jnp.int32, (TILE, TILE), 1)
    upper = lane >= row
    before = [jnp.zeros((TILE, TILE), f32)] * 2
    for offset in range(span + 1):
        for part in range(2):
            if offset < span:
                taps = taps_ref[part : part + 1, offset * TILE : (offset + 1) * TILE]
                rolled = pltpu.roll(
                    jnp.broadcast_to(taps, (TILE, TILE)), 0, 1, stride=1, stride_axis=0
                )
            else:
                rolled = jnp.zeros((TILE, TILE), f32)
            table = jnp.where(upper, rolled, before[part])
            before[part] = rolled
            high, low = split(table)
            for ref, value in ((high_ref, high), (low_ref, low)):
                if part == 0:
                    ref[offset, :TILE, :TILE] = value
                    ref[offset, TILE:, TILE:] = value
                else:
                    ref[offset, :TILE, TILE:] = value
                    ref[offset, TILE:, :TILE] = -value


def make_weights(plan_ref, steer_ref, high_ref, low_ref, wide, cut):
    per_beam = plan_ref.shape[0]
    sub, width = steer_ref.shape[2:]
    beam_blocks = steer_ref.shape[0] // per_beam
    beams = beam_blocks * width
    total = wide.shape[0] // 2
    first = lax.axis_index("pulse") * beam_blocks
    column = lax.broadcasted_iota(jnp.int32, plan_ref.shape, 1)
    for i in range(beam_blocks):
        mine = jnp.sum(jnp.where(column == first + i, plan_ref[...], 0), axis=1, keepdims=True)
        chosen = [mine[k : k + 1] for k in range(per_beam)]
        left = slice(i * width, (i + 1) * width)
        right = slice(beams + i * width, beams + (i + 1) * width)
        for block in range(total // sub):
            real = imag = jnp.zeros((sub, width), f32)
            for k in range(per_beam):
                here = jnp.broadcast_to(chosen[k] == block, (sub, width))
                real = jnp.where(here, steer_ref[i * per_beam + k, 0], real)
                imag = jnp.where(here, steer_ref[i * per_beam + k, 1], imag)
            start = block * sub
            if start < cut:
                re_row, im_row = start, start + cut
            else:
                re_row, im_row = start + cut, start + total
            wide[re_row : re_row + sub, left] = real
            wide[im_row : im_row + sub, left] = -imag
            wide[re_row : re_row + sub, right] = imag
            wide[im_row : im_row + sub, right] = real
    high, low = split(wide[...].T)
    high_ref[...] = high
    low_ref[...] = low


def place(value, block, part, xh, xl):
    rows = value.shape[0]
    high, low = split(value)
    at = (slice(block * rows, (block + 1) * rows), slice(part * TILE, (part + 1) * TILE))
    xh[at] = high
    xl[at] = low


def product(xh, xl, at, high, low):
    return dot(xh[at, :], high) + dot(xl[at, :], high) + dot(xh[at, :], low)


def inner(own_ref, high_ref, low_ref, out_ref, xh, xl):
    rows, blocks = own_ref.shape[1:3]
    span = high_ref.shape[0] - 1
    for part in range(2):
        value = jnp.swapaxes(own_ref[part], 0, 1)
        for block in range(blocks):
            place(value[block], block, part, xh, xl)
    at = slice(0, blocks * rows)
    out_ref[...] = product(xh, xl, at, high_ref[0], low_ref[0])
    for offset in range(1, min(span + 1, blocks)):
        at = slice(0, (blocks - offset) * rows)
        out_ref[offset * rows :, :] += product(xh, xl, at, high_ref[offset], low_ref[offset])


def outer(even_ref, first_row, odd_ref, high_ref, low_ref, out_ref, xh, xl):
    rows, span = odd_ref.shape[1:3]
    index = lax.axis_index("range")
    odd = lax.rem(index, 2) == 1
    for part in range(2):
        value = jnp.where(odd, even_ref[part, first_row : first_row + rows], odd_ref[part])
        value = jnp.swapaxes(jnp.where(index == 0, 0.0, value), 0, 1)
        for block in range(span):
            place(value[block], block, part, xh, xl)
    for offset in range(1, span + 1):
        at = slice((span - offset) * rows, span * rows)
        out_ref[: offset * rows, :] += product(xh, xl, at, high_ref[offset], low_ref[offset])


def columns(ref, blocks, yh, yl):
    rows = ref.shape[0] // blocks
    for block in range(blocks):
        lanes = slice(block * TILE, (block + 1) * TILE)
        for part in range(2):
            value = ref[block * rows : (block + 1) * rows, part * TILE : (part + 1) * TILE]
            high, low = split(value)
            yh[part * rows : (part + 1) * rows, lanes] = high
            yl[part * rows : (part + 1) * rows, lanes] = low


def share(wh, wl, at, yh, yl, lanes):
    left = jnp.concatenate([wh[:, at], wh[:, at], wl[:, at]], axis=1)
    right = jnp.concatenate([yh[:, lanes], yl[:, lanes], yh[:, lanes]], axis=0)
    return dot(left, right)


def send(shift, dense, out_ref, start, stop, sems):
    count = dense.shape[0] // 2
    pulses = out_ref.shape[3]
    pulse = lax.rem(lax.axis_index("pulse") + pulses - shift, pulses)
    copies = []
    for block in range(start, stop):
        for part in range(2):
            copy = pltpu.make_async_copy(
                dense.at[part * count : (part + 1) * count, block * TILE : (block + 1) * TILE],
                out_ref.at[part, :, block, pulse, :],
                sems.at[2 * block + part],
            )
            copy.start()
            copies.append(copy)
    return copies


def prepare_kernel(taps, rest, th, tl, partial, xh, xl):
    make_tables(taps, th, tl)
    inner(rest, th, tl, partial, xh, xl)


def rest_kernel(cut, even, odd, partial, th, tl, out, xh, xl):
    out[...] = partial[...]
    outer(even, cut, odd, th, tl, out, xh, xl)


def own_kernel(others, plan, steer, even, odd, own, rest, th, tl, *refs):
    raws, (out, wh, wl), partials = refs[:others], refs[others : others + 3], refs[others + 3 : 2 * others + 3]
    first, xh, xl, ah, al, bh, bl, dense, sems, wide = refs[2 * others + 3 :]
    blocks = out.shape[2]
    cut = own.shape[1]
    make_weights(plan, steer, wh, wl, wide, cut)
    columns(rest, blocks, bh, bl)
    inner(own, th, tl, first, xh, xl)
    outer(even, 0, odd, th, tl, first, xh, xl)
    columns(first, blocks, ah, al)
    copies = []
    for block in range(0, blocks, 2):
        lanes = slice(block * TILE, (block + 2) * TILE)
        dense[:, lanes] = share(wh, wl, slice(0, 2 * cut), ah, al, lanes)
        dense[:, lanes] += share(wh, wl, slice(2 * cut, None), bh, bl, lanes)
        copies += send(0, dense, out, block, block + 2, sems)
    for raw, partial in zip(raws, partials):
        inner(raw, th, tl, partial, xh, xl)
    for copy in copies:
        copy.wait()


def share_kernel(cut, blocks, rest, wh, wl, out, bh, bl):
    columns(rest, blocks, bh, bl)
    for block in range(0, blocks, 2):
        lanes = slice(block * TILE, (block + 2) * TILE)
        out[:, lanes] = share(wh, wl, slice(2 * cut, None), bh, bl, lanes)


def other_kernel(shift, part, odd, even, partial, th, tl, wh, wl, held, out, *refs):
    first, xh, xl, ah, al, dense, sems = refs
    blocks = out.shape[2]
    first[...] = partial[...]
    outer(even, 0, odd, th, tl, first, xh, xl)
    columns(first, blocks, ah, al)
    copies = []
    for block in range(0, blocks, 2):
        lanes = slice(block * TILE, (block + 2) * TILE)
        dense[:, lanes] = share(wh, wl, slice(0, ah.shape[0]), ah, al, lanes) + part[:, lanes]
        copies += send(shift, dense, out, block, block + 2, sems)
    for copy in copies:
        copy.wait()


def call(kernel, name, out_shape, in_specs, out_specs, scratch_shapes, flops=1000, **kwargs):
    return pl.pallas_call(
        kernel,
        out_shape=out_shape,
        in_specs=in_specs,
        out_specs=out_specs,
        scratch_shapes=scratch_shapes,
        name=name,
        compiler_params=pltpu.CompilerParams(vmem_limit_bytes=16 << 20),
        cost_estimate=pl.CostEstimate(flops=flops, bytes_accessed=1000, transcendentals=0),
        **kwargs,
    )


def body(echoes, steer_blocks, plan, filter_taps):
    pulses = lax.axis_size("pulse")
    subarrays, gates = echoes.shape[1], echoes.shape[3]
    blocks = gates // TILE
    span = filter_taps.shape[1] // TILE
    assert echoes.shape[2] == 1 and blocks >= span and lax.axis_size("range") % 4 == 0
    cut = subarrays // 2
    left = subarrays - cut
    depth = 2 * subarrays
    count = steer_blocks.shape[0] // plan.shape[1] * steer_blocks.shape[2]
    any_space = pl.BlockSpec(memory_space=pl.ANY)

    def shape(*dims, dtype=f32):
        return jax.ShapeDtypeStruct(dims, dtype)

    def halves(rows):
        return [pltpu.VMEM((blocks * rows, 2 * TILE), bf16)] * 2

    def columns_of(rows):
        return [pltpu.VMEM((2 * rows, gates), bf16)] * 2

    out_shape = shape(2, count, blocks, pulses, TILE)
    dense = [pltpu.VMEM((2 * count, gates), f32), pltpu.SemaphoreType.DMA((2 * blocks,))]

    samples = echoes.reshape(2, subarrays, blocks, TILE)
    tail = slice(blocks - span, blocks)
    raw, rest = samples[:, :cut], samples[:, cut:]
    odd_rest = from_odd(rest[:, :, tail])
    others_raw = [shifted(raw, "pulse", k) for k in range(1, pulses)]
    even = from_even(samples[:, :, tail])
    odd_raw = from_odd(raw[:, :, tail])

    *tables, partial_rest = call(
        prepare_kernel,
        "prepare",
        [shape(span + 1, 2 * TILE, 2 * TILE, dtype=bf16)] * 2 + [shape(blocks * left, 2 * TILE)],
        [VMEM] * 2,
        [VMEM] * 3,
        halves(left),
    )(filter_taps, rest)
    own_rest = call(
        functools.partial(rest_kernel, cut),
        "rest",
        shape(blocks * left, 2 * TILE),
        [VMEM] * 5,
        VMEM,
        halves(left),
    )(even, odd_rest, partial_rest, *tables)
    others_rest = [shifted(own_rest, "pulse", k) for k in range(1, pulses)]
    others_raw, own_rest = lax.optimization_barrier((others_raw, own_rest))
    odd_others = [from_odd(r[:, :, tail]) for r in others_raw]
    even_others = [from_even(r[:, :, tail]) for r in others_raw]
    out, *made = call(
        functools.partial(own_kernel, pulses - 1),
        "own",
        [out_shape]
        + [shape(2 * count, depth, dtype=bf16)] * 2
        + [shape(blocks * cut, 2 * TILE)] * (pulses - 1),
        [VMEM] * (7 + pulses),
        [any_space] + [VMEM] * (1 + pulses),
        [
            pltpu.VMEM((blocks * cut, 2 * TILE), f32),
            *halves(cut),
            *columns_of(cut),
            *columns_of(left),
            *dense,
            pltpu.VMEM((depth, 2 * count), f32),
        ],
    )(plan.T, steer_blocks.transpose(0, 1, 3, 2), even, odd_raw, raw, own_rest, *tables, *others_raw)
    weights, partials = made[:2], made[2:]
    for k in range(1, pulses):
        part = call(
            functools.partial(share_kernel, cut, blocks),
            "share",
            shape(2 * count, gates),
            [VMEM] * 3,
            VMEM,
            columns_of(left),
            flops=1 << 36,
        )(others_rest[k - 1], *weights)
        out = call(
            functools.partial(other_kernel, k),
            "other",
            out_shape,
            [VMEM] * 8 + [any_space],
            any_space,
            [pltpu.VMEM((blocks * cut, 2 * TILE), f32), *halves(cut), *columns_of(cut), *dense],
            input_output_aliases={8: 0},
        )(part, odd_others[k - 1], even_others[k - 1], partials[k - 1], *tables, *weights, out)
    return out.transpose(0, 1, 3, 2, 4).reshape(2, count, pulses, gates)


def solution(mesh):
    in_specs = (P(None, None, "pulse", "range"), P("pulse", None, None, None), P(), P())
    out_specs = P(None, "pulse", None, "range")
    return jax.shard_map(body, mesh=mesh, in_specs=in_specs, out_specs=out_specs, check_vma=False)
```

profile of v0, /device:TPU:0, one launch (start us, length us, event | category | flops | bytes accessed | tf_op | source)
XLA Modules:
  0.0 20.7 jit_solution(2017074783065175711)
XLA Ops:
  0.0 0.5 %collective-permute-start = (f32[2,64,8,128]{3,2,1,0:T(8,128)}, f32[2,64,8,128]{3,2,1,0:T(8,128)S(1)}, u32[]{:S(2)}, u32[]{:S(2)}) collective-permute-start(f32[2,64,8,128]{3,2,1,0:T(8,128)} %bitcast.8), channel_id=1, source_target_pairs={{0,2},{2,0},{4,6},{6,4},{8,10},{10,8},{12,14},{14,12},{16,18},{18,... | collective-permute-start | bytes 1572872 | tf_op jit(solution)/shard_map/ppermute | solution.py:44
  0.5 0.0 copy-start.2
  0.5 1.1 %fusion = (f32[2,32,8,128]{3,2,1,0:T(8,128)S(1)}, f32[2,32,8,128]{3,2,1,0:T(8,128)S(1)}) fusion(f32[2,64,8,128]{3,2,1,0:T(8,128)} %bitcast.9), kind=kLoop, calls=%fused_computation | loop fusion | bytes 1048576 | tf_op jit(solution)/shard_map/slice | solution.py:275
  1.5 0.0 copy-start
  1.5 0.1 collective-permute-start.1
  1.7 2.9 %collective-permute-start.4 = (f32[2,32,8,128]{3,2,1,0:T(8,128)S(1)}, f32[2,32,8,128]{3,2,1,0:T(8,128)S(1)}, u32[]{:S(2)}, u32[]{:S(2)}) collective-permute-start(f32[2,32,8,128]{3,2,1,0:T(8,128)S(1)} %get-tuple-element.23.own), channel_id=1, source_target_pairs={{0,1},{1,0},{2,3},{3,2},{4,5},{5,4},{6,7},{7,6},{8,9},{9,8},{10,11... | collective-permute-start | bytes 786440 | tf_op jit(solution)/shard_map/ppermute | solution.py:28
  4.6 0.8 %collective-permute-start.3 = (f32[2,32,8,128]{3,2,1,0:T(8,128)S(1)}, f32[2,32,8,128]{3,2,1,0:T(8,128)S(1)}, u32[]{:S(2)}, u32[]{:S(2)}) collective-permute-start(f32[2,32,8,128]{3,2,1,0:T(8,128)S(1)} %get-tuple-element.23.own), channel_id=1, source_target_pairs={{0,2},{2,4},{4,0},{6,8},{8,10},{10,12},{12,6},{14,16},{16,18},{18,... | collective-permute-start | bytes 786440 | tf_op jit(solution)/shard_map/ppermute | solution.py:39
  5.5 0.0 copy-start.1
  5.5 0.7 %copy-done.1 = f32[2,1024]{1,0:T(2,128)S(1)} copy-done((f32[2,1024]{1,0:T(2,128)S(1)}, f32[2,1024]{1,0:T(2,128)}, u32[]{:S(2)}) %copy-start.1) | copy-done | bytes 8216
  6.1 1.0 %prepare.1 = (bf16[9,256,256]{2,1,0:T(8,128)(2,1)S(1)}, bf16[9,256,256]{2,1,0:T(8,128)(2,1)S(1)}, f32[256,256]{1,0:T(8,128)S(1)}) custom-call(f32[2,1024]{1,0:T(2,128)S(1)} %copy-done.1, f32[2,32,8,128]{3,2,1,0:T(8,128)S(1)} %get-tuple-element.24.rest), custom_call_target="tpu_custom_call" | custom-call | flops 1000 | bytes 1000 | tf_op jit(solution)/shard_map/prepare/pallas_call | solution.py:281
  7.2 1.3 %collective-permute-done.1.odd = f32[2,32,8,128]{3,2,1,0:T(8,128)S(1)} collective-permute-done((f32[2,32,8,128]{3,2,1,0:T(8,128)S(1)}, f32[2,32,8,128]{3,2,1,0:T(8,128)S(1)}, u32[]{:S(2)}, u32[]{:S(2)}) %collective-permute-start.1) | collective-permute-done | bytes 262176 | tf_op jit(solution)/shard_map/ppermute | solution.py:39
  8.5 0.0 collective-permute-done.even
  8.5 0.8 %rest.1 = f32[256,256]{1,0:T(8,128)S(1)} custom-call(f32[2,64,8,128]{3,2,1,0:T(8,128)S(1)} %collective-permute-done.even, f32[2,32,8,128]{3,2,1,0:T(8,128)S(1)} %collective-permute-done.1.odd, f32[256,256]{1,0:T(8,128)S(1)} %get-tuple-element.14.partial, bf16[9,256,256]{2,1,0:T(8,128)(2,1)S(1)} %get-tuple-element.15.th, ...), custom_call_target="tpu_custom_call" | custom-call | flops 1000 | bytes 1000 | tf_op jit(solution)/shard_map/rest/pallas_call | solution.py:289
  9.3 2.1 %collective-permute-start.2 = (f32[256,256]{1,0:T(8,128)S(1)}, f32[256,256]{1,0:T(8,128)S(1)}, u32[]{:S(2)}, u32[]{:S(2)}) collective-permute-start(f32[256,256]{1,0:T(8,128)S(1)} %rest.1), channel_id=1, source_target_pairs={{0,1},{1,0},{2,3},{3,2},{4,5},{5,4},{6,7},{7,6},{8,9},{9,8},{10,11... | collective-permute-start | bytes 786440 | tf_op jit(solution)/shard_map/ppermute | solution.py:28
  11.3 0.0 collective-permute-done.4.refs_0_
  11.3 0.3 %collective-permute-start.6 = (f32[2,32,8,128]{3,2,1,0:T(8,128)S(1)}, f32[2,32,8,128]{3,2,1,0:T(8,128)S(1)}, u32[]{:S(2)}, u32[]{:S(2)}) collective-permute-start(f32[2,32,8,128]{3,2,1,0:T(8,128)S(1)} %collective-permute-done.4.refs_0_), channel_id=1, source_target_pairs={{0,2},{2,0},{4,6},{6,4},{8,10},{10,8},{12,14},{14,12},{16,18},{18,... | collective-permute-start | bytes 786440 | tf_op jit(solution)/shard_map/ppermute | solution.py:44
  11.6 0.2 %collective-permute-start.5 = (f32[2,32,8,128]{3,2,1,0:T(8,128)S(1)}, f32[2,32,8,128]{3,2,1,0:T(8,128)S(1)}, u32[]{:S(2)}, u32[]{:S(2)}) collective-permute-start(f32[2,32,8,128]{3,2,1,0:T(8,128)S(1)} %collective-permute-done.4.refs_0_), channel_id=1, source_target_pairs={{0,2},{2,4},{4,0},{6,8},{8,10},{10,12},{12,6},{14,16},{16,18},{18,... | collective-permute-start | bytes 786440 | tf_op jit(solution)/shard_map/ppermute | solution.py:39
  11.8 0.0 collective-permute-done.3.odd
  11.8 0.0 copy-done.2
  11.8 0.0 copy-done
  11.8 4.7 %own.1 = (f32[2,128,8,2,128]{4,3,2,1,0:T(2,128)}, bf16[256,128]{1,0:T(8,128)(2,1)S(1)}, bf16[256,128]{1,0:T(8,128)(2,1)S(1)}, f32[256,256]{1,0:T(8,128)S(1)}) custom-call(s32[4,8]{1,0:T(4,128)S(1)} %bitcast.7, f32[16,2,8,32]{3,2,1,0:T(8,128)S(1)} %bitcast.6, f32[2,64,8,128]{3,2,1,0:T(8,128)S(1)} %collective-permute-done.even, ...), custom_call_target="tpu_custom_call" | custom-call | flops 1000 | bytes 1000 | tf_op jit(solution)/shard_map/own/pallas_call | solution.py:301
  16.6 0.8 %collective-permute-done.2.rest = f32[256,256]{1,0:T(8,128)S(1)} collective-permute-done((f32[256,256]{1,0:T(8,128)S(1)}, f32[256,256]{1,0:T(8,128)S(1)}, u32[]{:S(2)}, u32[]{:S(2)}) %collective-permute-start.2) | collective-permute-done | bytes 262176 | tf_op jit(solution)/shard_map/ppermute | solution.py:28
  17.4 0.4 %share.1.part = f32[256,1024]{1,0:T(8,128)S(1)} custom-call(f32[256,256]{1,0:T(8,128)S(1)} %collective-permute-done.2.rest, bf16[256,128]{1,0:T(8,128)(2,1)S(1)} %get-tuple-element.19.wh, bf16[256,128]{1,0:T(8,128)(2,1)S(1)} %get-tuple-element.20.wl), custom_call_target="tpu_custom_call" | custom-call | flops 68719476736 | bytes 1000 | tf_op jit(solution)/shard_map/share/pallas_call | solution.py:320
  17.7 0.0 collective-permute-done.6.even
  17.8 0.2 collective-permute-done.5.odd
  18.0 2.7 %other.1 = f32[2,128,8,2,128]{4,3,2,1,0:T(2,128)} custom-call(f32[256,1024]{1,0:T(8,128)S(1)} %share.1.part, f32[2,32,8,128]{3,2,1,0:T(8,128)S(1)} %collective-permute-done.5.odd, f32[2,32,8,128]{3,2,1,0:T(8,128)S(1)} %collective-permute-done.6.even, f32[256,256]{1,0:T(8,128)S(1)} %get-tuple-element.21.partial, ...), custom_call_target="tpu_custom_call", output_to_operand_aliasing={{}: (8, {})} | custom-call | flops 1000 | bytes 1000 | tf_op jit(solution)/shard_map/other/pallas_call | solution.py:329
Async XLA Ops:
  0.0 8.5 %collective-permute-start = (f32[2,64,8,128]{3,2,1,0:T(8,128)}, f32[2,64,8,128]{3,2,1,0:T(8,128)S(1)}, u32[]{:S(2)}, u32[]{:S(2)}) collective-permute-start(f32[2,64,8,128]{3,2,1,0:T(8,128)} %bitcast.8), channel_id=1, source_target_pairs={{0,2},{2,0},{4,6},{6,4},{8,10},{10,8},{12,14},{14,12},{16,18},{18,... | collective-permute-start | bytes 1572872 | tf_op jit(solution)/shard_map/ppermute | solution.py:44
  0.5 11.4 %copy-start.2 = (s32[8,4]{0,1:T(4,128)S(1)}, s32[8,4]{0,1:T(4,128)}, u32[]{:S(2)}) copy-start(s32[8,4]{0,1:T(4,128)} %param.6) | copy-start | bytes 388
  1.5 10.3 %copy-start = (f32[16,2,32,8]{2,3,1,0:T(8,128)S(1)}, f32[16,2,32,8]{2,3,1,0:T(8,128)}, u32[]{:S(2)}) copy-start(f32[16,2,32,8]{2,3,1,0:T(8,128)} %param.5) | copy-start | bytes 98308
  1.5 6.9 %collective-permute-start.1 = (f32[2,32,8,128]{3,2,1,0:T(8,128)S(1)}, f32[2,32,8,128]{3,2,1,0:T(8,128)S(1)}, u32[]{:S(2)}, u32[]{:S(2)}) collective-permute-start(f32[2,32,8,128]{3,2,1,0:T(8,128)S(1)} %get-tuple-element.24.rest), channel_id=1, source_target_pairs={{0,2},{2,4},{4,0},{6,8},{8,10},{10,12},{12,6},{14,16},{16,18},{18,... | collective-permute-start | bytes 786440 | tf_op jit(solution)/shard_map/ppermute | solution.py:39
  1.7 9.7 %collective-permute-start.4 = (f32[2,32,8,128]{3,2,1,0:T(8,128)S(1)}, f32[2,32,8,128]{3,2,1,0:T(8,128)S(1)}, u32[]{:S(2)}, u32[]{:S(2)}) collective-permute-start(f32[2,32,8,128]{3,2,1,0:T(8,128)S(1)} %get-tuple-element.23.own), channel_id=1, source_target_pairs={{0,1},{1,0},{2,3},{3,2},{4,5},{5,4},{6,7},{7,6},{8,9},{9,8},{10,11... | collective-permute-start | bytes 786440 | tf_op jit(solution)/shard_map/ppermute | solution.py:28
  4.6 7.2 %collective-permute-start.3 = (f32[2,32,8,128]{3,2,1,0:T(8,128)S(1)}, f32[2,32,8,128]{3,2,1,0:T(8,128)S(1)}, u32[]{:S(2)}, u32[]{:S(2)}) collective-permute-start(f32[2,32,8,128]{3,2,1,0:T(8,128)S(1)} %get-tuple-element.23.own), channel_id=1, source_target_pairs={{0,2},{2,4},{4,0},{6,8},{8,10},{10,12},{12,6},{14,16},{16,18},{18,... | collective-permute-start | bytes 786440 | tf_op jit(solution)/shard_map/ppermute | solution.py:39
  5.5 0.7 %copy-start.1 = (f32[2,1024]{1,0:T(2,128)S(1)}, f32[2,1024]{1,0:T(2,128)}, u32[]{:S(2)}) copy-start(f32[2,1024]{1,0:T(2,128)} %taps.1) | copy-start | bytes 24580
  9.3 8.1 %collective-permute-start.2 = (f32[256,256]{1,0:T(8,128)S(1)}, f32[256,256]{1,0:T(8,128)S(1)}, u32[]{:S(2)}, u32[]{:S(2)}) collective-permute-start(f32[256,256]{1,0:T(8,128)S(1)} %rest.1), channel_id=1, source_target_pairs={{0,1},{1,0},{2,3},{3,2},{4,5},{5,4},{6,7},{7,6},{8,9},{9,8},{10,11... | collective-permute-start | bytes 786440 | tf_op jit(solution)/shard_map/ppermute | solution.py:28
  11.3 6.4 %collective-permute-start.6 = (f32[2,32,8,128]{3,2,1,0:T(8,128)S(1)}, f32[2,32,8,128]{3,2,1,0:T(8,128)S(1)}, u32[]{:S(2)}, u32[]{:S(2)}) collective-permute-start(f32[2,32,8,128]{3,2,1,0:T(8,128)S(1)} %collective-permute-done.4.refs_0_), channel_id=1, source_target_pairs={{0,2},{2,0},{4,6},{6,4},{8,10},{10,8},{12,14},{14,12},{16,18},{18,... | collective-permute-start | bytes 786440 | tf_op jit(solution)/shard_map/ppermute | solution.py:44
  11.6 6.4 %collective-permute-start.5 = (f32[2,32,8,128]{3,2,1,0:T(8,128)S(1)}, f32[2,32,8,128]{3,2,1,0:T(8,128)S(1)}, u32[]{:S(2)}, u32[]{:S(2)}) collective-permute-start(f32[2,32,8,128]{3,2,1,0:T(8,128)S(1)} %collective-permute-done.4.refs_0_), channel_id=1, source_target_pairs={{0,2},{2,4},{4,0},{6,8},{8,10},{10,12},{12,6},{14,16},{16,18},{18,... | collective-permute-start | bytes 786440 | tf_op jit(solution)/shard_map/ppermute | solution.py:39
where the time goes:
time: 20.9 us; the launch traced here: 20.7 us
  Pallas kernels  9.62 us (46%)
  starting transfers between devices  6.92 us (33%)
  waiting for transfers between devices  2.29 us (11%)
  local copies, waits for them, and re-layouts  1.78 us (9%)
    ppermute x2, starting transfers between devices, shifted(): lax.ppermute(value, axis, [(i, (i + steps) % count) for i in range(count)])  4.99 us
    pallas_call x1, Pallas kernels, body(): call(functools.partial(own_kernel, pulses - 1), 'own', [out_shape] + [sha...  4.75 us
    pallas_call x1, Pallas kernels, body(): call(functools.partial(other_kernel, k), 'other', out_shape, [VMEM] * 8 +...  2.72 us
    ppermute x3, waiting for transfers between devices, from_odd(): return lax.ppermute(value, 'range', list(target.items()))  1.5 us
    ppermute x3, starting transfers between devices, from_odd(): return lax.ppermute(value, 'range', list(target.items()))  1.21 us
    slice x1, local copies, waits for them, and re-layouts, body(): raw, rest = (samples[:, :cut], samples[:, cut:])  1.08 us
    pallas_call x1, Pallas kernels, body(): call(prepare_kernel, 'prepare', [shape(span + 1, 2 * TILE, 2 * TILE, dtyp...  1.02 us
    ppermute x2, waiting for transfers between devices, shifted(): lax.ppermute(value, axis, [(i, (i + steps) % count) for i in range(count)])  0.78 us
  transfers between devices with their start and end apart: 7, of which 3 were waited for; matrix products, arithmetic and copies ran while one was open for 5% of the time, Pallas kernels for 33%

commit v1 on v0

v1 whole, which is shorter than its diff:
```python
import functools

import jax
import jax.numpy as jnp
from jax import lax
from jax.experimental import pallas as pl
from jax.experimental.pallas import tpu as pltpu
from jax.sharding import PartitionSpec as P

TILE = 128
f32 = jnp.float32
bf16 = jnp.bfloat16
VMEM = pl.BlockSpec(memory_space=pltpu.VMEM)
SMEM = pl.BlockSpec(memory_space=pltpu.SMEM)


def dot(left, right):
    return jnp.dot(left, right, preferred_element_type=f32)


def split(value):
    high = value.astype(bf16)
    return high, (value - high.astype(f32)).astype(bf16)


def shifted(value, axis, steps):
    count = lax.axis_size(axis)
    return lax.ppermute(value, axis, [(i, (i + steps) % count) for i in range(count)])


def from_odd(value):
    count = lax.axis_size("range")
    target = {i: (i + 1) % count for i in range(count)}
    source, goal = count - 1, count - 5
    while goal > 0:
        target[source] = goal
        source, goal = goal - 1, goal - 4
    target[source] = 0
    return lax.ppermute(value, "range", list(target.items()))


def from_even(value):
    count = lax.axis_size("range")
    return lax.ppermute(value, "range", [(i, i ^ 1) for i in range(count)])


def make_tables(taps_ref, high_ref, low_ref):
    span = taps_ref.shape[1] // TILE
    row = lax.broadcasted_iota(jnp.int32, (TILE, TILE), 0)
    lane = lax.broadcasted_iota(jnp.int32, (TILE, TILE), 1)
    upper = lane >= row
    before = [jnp.zeros((TILE, TILE), f32)] * 2
    for offset in range(span + 1):
        for part in range(2):
            if offset < span:
                taps = taps_ref[part : part + 1, offset * TILE : (offset + 1) * TILE]
                rolled = pltpu.roll(
                    jnp.broadcast_to(taps, (TILE, TILE)), 0, 1, stride=1, stride_axis=0
                )
            else:
                rolled = jnp.zeros((TILE, TILE), f32)
            table = jnp.where(upper, rolled, before[part])
            before[part] = rolled
            high, low = split(table)
            for ref, value in ((high_ref, high), (low_ref, low)):
                if part == 0:
                    ref[offset, :TILE, :TILE] = value
                    ref[offset, TILE:, TILE:] = value
                else:
                    ref[offset, :TILE, TILE:] = value
                    ref[offset, TILE:, :TILE] = -value


def make_weights(plan_ref, steer_ref, outs, wide, groups):
    per_beam = plan_ref.shape[0]
    sub, width = steer_ref.shape[2:]
    beam_blocks = steer_ref.shape[0] // per_beam
    beams = beam_blocks * width
    first = lax.axis_index("pulse") * beam_blocks
    column = lax.broadcasted_iota(jnp.int32, plan_ref.shape, 1)
    for i in range(beam_blocks):
        mine = jnp.sum(jnp.where(column == first + i, plan_ref[...], 0), axis=1, keepdims=True)
        chosen = [mine[k : k + 1] for k in range(per_beam)]
        left = slice(i * width, (i + 1) * width)
        right = slice(beams + i * width, beams + (i + 1) * width)
        for at, size in groups:
            for start in range(at, at + size, sub):
                real = imag = jnp.zeros((sub, width), f32)
                for k in range(per_beam):
                    here = jnp.broadcast_to(chosen[k] == start // sub, (sub, width))
                    real = jnp.where(here, steer_ref[i * per_beam + k, 0], real)
                    imag = jnp.where(here, steer_ref[i * per_beam + k, 1], imag)
                re_row = at + start
                im_row = re_row + size
                wide[re_row : re_row + sub, left] = real
                wide[im_row : im_row + sub, left] = -imag
                wide[re_row : re_row + sub, right] = imag
                wide[im_row : im_row + sub, right] = real
    for ref, (at, size) in zip(outs, groups):
        high, low = split(wide[2 * at : 2 * (at + size), :].T)
        ref[...] = jnp.concatenate([high, high, low], axis=1)


def place(value, xh, xl, part):
    blocks, rows = value.shape[:2]
    for block in range(blocks):
        high, low = split(value[block])
        at = (slice(block * rows, (block + 1) * rows), slice(part * TILE, (part + 1) * TILE))
        xh[at] = high
        xl[at] = low


def product(xh, xl, at, high, low):
    return dot(xh[at, :], high) + dot(xl[at, :], high) + dot(xh[at, :], low)


def inner(own_ref, high_ref, low_ref, out_ref, xh, xl):
    rows, blocks = own_ref.shape[1:3]
    span = high_ref.shape[0] - 1
    for part in range(2):
        place(jnp.swapaxes(own_ref[part], 0, 1), xh, xl, part)
    at = slice(0, blocks * rows)
    out_ref[...] = product(xh, xl, at, high_ref[0], low_ref[0])
    for offset in range(1, min(span + 1, blocks)):
        at = slice(0, (blocks - offset) * rows)
        out_ref[offset * rows :, :] += product(xh, xl, at, high_ref[offset], low_ref[offset])


def spill(high_ref, low_ref, out_ref, xh, xl):
    span = high_ref.shape[0] - 1
    rows = xh.shape[0] // span
    for offset in range(1, span + 1):
        at = slice((span - offset) * rows, span * rows)
        out_ref[: offset * rows, :] += product(xh, xl, at, high_ref[offset], low_ref[offset])


def outer(even_ref, start, odd_ref, high_ref, low_ref, out_ref, xh, xl):
    rows, span = odd_ref.shape[1:3]
    index = lax.axis_index("range")
    odd = lax.rem(index, 2) == 1
    for part in range(2):
        value = jnp.where(odd, even_ref[part, start : start + rows], odd_ref[part])
        place(jnp.swapaxes(jnp.where(index == 0, 0.0, value), 0, 1), xh, xl, part)
    spill(high_ref, low_ref, out_ref, xh, xl)


def columns(ref, y):
    blocks = y.shape[1] // TILE
    rows = y.shape[0] // 6
    for block in range(blocks):
        lanes = slice(block * TILE, (block + 1) * TILE)
        for part in range(2):
            high, low = split(ref[block * rows : (block + 1) * rows, part * TILE : (part + 1) * TILE])
            for copy, value in enumerate((high, low, high)):
                base = (2 * copy + part) * rows
                y[base : base + rows, lanes] = value


def send(shift, dense, out_ref, start, stop, sems):
    count = dense.shape[0] // 2
    pulses = out_ref.shape[3]
    pulse = lax.rem(lax.axis_index("pulse") + pulses - shift, pulses)
    copies = []
    for block in range(start, stop):
        for part in range(2):
            copy = pltpu.make_async_copy(
                dense.at[part * count : (part + 1) * count, block * TILE : (block + 1) * TILE],
                out_ref.at[part, :, block, pulse, :],
                sems.at[2 * block + part],
            )
            copy.start()
            copies.append(copy)
    return copies


def parts_of(blocks):
    half = -(-blocks // 2)
    return [(0, half), (half, blocks)] if half < blocks else [(0, blocks)]


def prepare_kernel(taps, raw, rest, th, tl, raw_partial, rest_partial, *scratch):
    make_tables(taps, th, tl)
    inner(rest, th, tl, rest_partial, *scratch[:2])
    inner(raw, th, tl, raw_partial, *scratch[2:])


def rest_kernel(cut, even, odd, partial, th, tl, out, xh, xl):
    rows = partial.shape[0]
    out[:rows, :] = partial[...]
    out[rows:, :] = jnp.zeros((out.shape[0] - rows, out.shape[1]), f32)
    outer(even, cut, odd, th, tl, out, xh, xl)


def own_kernel(groups, others, plan, steer, even, odd, partial, rest, th, tl, *refs):
    raws, (out, wa, wb), partials = refs[:others], refs[others : others + 3], refs[others + 3 : 2 * others + 3]
    first, xh, xl, ya, yb, dense, sems, wide = refs[2 * others + 3 :]
    make_weights(plan, steer, (wa, wb), wide, groups)
    columns(rest, yb)
    first[...] = partial[...]
    outer(even, 0, odd, th, tl, first, xh, xl)
    columns(first, ya)
    copies = []
    for start, stop in parts_of(out.shape[2]):
        lanes = slice(start * TILE, stop * TILE)
        dense[:, lanes] = dot(wa[...], ya[:, lanes]) + dot(wb[...], yb[:, lanes])
        copies += send(0, dense, out, start, stop, sems)
    for raw, result in zip(raws, partials):
        inner(raw, th, tl, result, xh, xl)
    for copy in copies:
        copy.wait()


def spill_kernel(parity, own, after, th, tl, out, xh, xl):
    span = th.shape[0] - 1

    @pl.when(lax.rem(lax.axis_index("range"), 2) == parity)
    def _():
        for part in range(2):
            place(jnp.swapaxes(own[part, :, own.shape[2] - span :], 0, 1), xh, xl, part)
        out[...] = jnp.zeros_like(out)
        spill(th, tl, out, xh, xl)


def ready_kernel(odd, rest, yb):
    columns(rest, yb)


def other_kernel(shift, yb, even, odd, partial, wa, wb, held, out, first, ya, dense, sems):
    index = lax.axis_index("range")
    count = even.shape[0]
    spilled = jnp.where(lax.rem(index, 2) == 1, even[...], odd[:count, :])
    spilled = jnp.where(index == 0, 0.0, spilled)
    first[...] = partial[...]
    first[:count, :] += spilled
    columns(first, ya)
    copies = []
    for start, stop in parts_of(out.shape[2]):
        lanes = slice(start * TILE, stop * TILE)
        dense[:, lanes] = dot(wa[...], ya[:, lanes]) + dot(wb[...], yb[:, lanes])
        copies += send(shift, dense, out, start, stop, sems)
    for copy in copies:
        copy.wait()


def call(kernel, name, out_shape, in_specs, out_specs, scratch_shapes, flops=1000, **kwargs):
    return pl.pallas_call(
        kernel,
        out_shape=out_shape,
        in_specs=in_specs,
        out_specs=out_specs,
        scratch_shapes=scratch_shapes,
        name=name,
        compiler_params=pltpu.CompilerParams(vmem_limit_bytes=16 << 20),
        cost_estimate=pl.CostEstimate(flops=flops, bytes_accessed=1000, transcendentals=0),
        **kwargs,
    )


def body(echoes, steer_blocks, plan, filter_taps):
    pulses = lax.axis_size("pulse")
    others = pulses - 1
    subarrays, gates = echoes.shape[1], echoes.shape[3]
    blocks = gates // TILE
    span = filter_taps.shape[1] // TILE
    assert echoes.shape[2] == 1 and blocks >= span and lax.axis_size("range") % 4 == 0
    cut = subarrays // 2
    left = subarrays - cut
    groups = ((0, cut), (cut, left))
    count = steer_blocks.shape[0] // plan.shape[1] * steer_blocks.shape[2]
    any_space = pl.BlockSpec(memory_space=pl.ANY)

    def shape(*dims, dtype=f32):
        return jax.ShapeDtypeStruct(dims, dtype)

    def halves(rows):
        return [pltpu.VMEM((blocks * rows, 2 * TILE), bf16)] * 2

    out_shape = shape(2, count, blocks, pulses, TILE)
    ya, yb = (pltpu.VMEM((6 * rows, gates), bf16) for rows in (cut, left))
    first = pltpu.VMEM((blocks * cut, 2 * TILE), f32)
    dense = [pltpu.VMEM((2 * count, gates), f32), pltpu.SemaphoreType.DMA((2 * blocks,))]

    samples = echoes.reshape(2, subarrays, blocks, TILE)
    tail = slice(blocks - span, blocks)
    raw, rest = samples[:, :cut], samples[:, cut:]
    odd_rest = from_odd(rest[:, :, tail])
    others_raw = [shifted(raw, "pulse", k) for k in range(1, pulses)]
    even = from_even(samples[:, :, tail])
    odd_raw = from_odd(raw[:, :, tail])

    th, tl, raw_partial, rest_partial = call(
        prepare_kernel,
        "prepare",
        [shape(span + 1, 2 * TILE, 2 * TILE, dtype=bf16)] * 2
        + [shape(blocks * rows, 2 * TILE) for rows in (cut, left)],
        [VMEM] * 3,
        [VMEM] * 4,
        [*halves(left), *halves(cut)],
    )(filter_taps, raw, rest)
    own_rest = call(
        functools.partial(rest_kernel, cut),
        "rest",
        shape(blocks * left + 8, 2 * TILE),
        [VMEM] * 5,
        VMEM,
        halves(left),
    )(even, odd_rest, rest_partial, th, tl)
    others_rest = [shifted(own_rest, "pulse", k) for k in range(1, pulses)]
    others_raw, own_rest = lax.optimization_barrier((others_raw, own_rest))
    def spilled(parity, raw, flops, more):
        return call(
            functools.partial(spill_kernel, parity),
            "spill",
            shape(span * cut + more, 2 * TILE),
            [VMEM, any_space, VMEM, VMEM],
            VMEM,
            [pltpu.VMEM((span * cut, 2 * TILE), bf16)] * 2,
            flops=flops,
        )(raw, own_rest, th, tl)

    odd_others = [from_odd(spilled(1, raw, 1 << 36, 0)) for raw in others_raw]
    even_others = [from_even(spilled(0, raw, 1000, 0)) for raw in others_raw]
    out, wa, wb, *partials = call(
        functools.partial(own_kernel, groups, others),
        "own",
        [out_shape]
        + [shape(2 * count, 6 * rows, dtype=bf16) for rows in (cut, left)]
        + [shape(blocks * cut, 2 * TILE)] * others,
        [VMEM] * (8 + others),
        [any_space] + [VMEM] * (2 + others),
        [first, *halves(cut), ya, yb, *dense, pltpu.VMEM((2 * subarrays, 2 * count), f32)],
    )(
        plan.T,
        steer_blocks.transpose(0, 1, 3, 2),
        even,
        odd_raw,
        raw_partial,
        own_rest,
        th,
        tl,
        *others_raw,
    )
    for k in range(1, pulses):
        ready = call(
            ready_kernel,
            "ready",
            shape(6 * left, gates, dtype=bf16),
            [any_space, VMEM],
            VMEM,
            [],
            flops=1 << 36,
        )(odd_others[k - 1], others_rest[k - 1])
        out = call(
            functools.partial(other_kernel, k),
            "other",
            out_shape,
            [VMEM] * 6 + [any_space],
            any_space,
            [first, ya, *dense],
            input_output_aliases={6: 0},
        )(ready, even_others[k - 1], odd_others[k - 1], partials[k - 1], wa, wb, out)
    return out.transpose(0, 1, 3, 2, 4).reshape(2, count, pulses, gates)


def solution(mesh):
    in_specs = (P(None, None, "pulse", "range"), P("pulse", None, None, None), P(), P())
    out_specs = P(None, "pulse", None, "range")
    return jax.shard_map(body, mesh=mesh, in_specs=in_specs, out_specs=out_specs, check_vma=False)
```

time: 20.9 us -> 19.6 us (0.938)
  Pallas kernels: 9.62 us -> 8.04 us
  starting transfers between devices: 6.92 us -> 7.56 us
  waiting for transfers between devices: 2.29 us -> 1.95 us
    pallas_call x4 -> x6, Pallas kernels: 8.6 us -> 6.51 us  [the longest x1 3.34 us: body(): call(functools.partial(own_kernel, groups, others), 'own', [out_shape] +...]
    ppermute x3, starting transfers between devices: 1.21 us -> 2.04 us  [from_odd(): return lax.ppermute(value, 'range', list(target.items()))]
    ppermute x2, waiting for transfers between devices: 0.78 us -> 0.01 us  [shifted(): lax.ppermute(value, axis, [(i, (i + steps) % count) for i in range(count)])]
    pallas_call x1, Pallas kernels: 1.02 us -> 1.53 us  [body(): call(prepare_kernel, 'prepare', [shape(span + 1, 2 * TILE, 2 * TILE, dtyp...]
    ppermute x3, waiting for transfers between devices: 1.5 us -> 1.94 us  [from_odd(): return lax.ppermute(value, 'range', list(target.items()))]
  transfers between devices with their start and end apart: 7 -> 7, of which waited for: 3 -> 2; matrix products, arithmetic and copies ran while one was open for 5% -> 5% of each run, Pallas kernels for 33% -> 33%
where the time goes in v1:
time: 19.6 us; the launch traced here: 19.4 us
  Pallas kernels  8.04 us (41%)
  starting transfers between devices  7.56 us (39%)
  waiting for transfers between devices  1.95 us (10%)
  local copies, waits for them, and re-layouts  1.77 us (9%)
    ppermute x2, starting transfers between devices, shifted(): lax.ppermute(value, axis, [(i, (i + steps) % count) for i in range(count)])  4.99 us
    pallas_call x1, Pallas kernels, body(): call(functools.partial(own_kernel, groups, others), 'own', [out_shape] +...  3.34 us
    ppermute x3, starting transfers between devices, from_odd(): return lax.ppermute(value, 'range', list(target.items()))  2.04 us
    ppermute x3, waiting for transfers between devices, from_odd(): return lax.ppermute(value, 'range', list(target.items()))  1.94 us
    pallas_call x1, Pallas kernels, body(): call(functools.partial(other_kernel, k), 'other', out_shape, [VMEM] * 6 +...  1.57 us
    pallas_call x1, Pallas kernels, body(): call(prepare_kernel, 'prepare', [shape(span + 1, 2 * TILE, 2 * TILE, dtyp...  1.53 us
    slice x1, local copies, waits for them, and re-layouts, body(): raw, rest = (samples[:, :cut], samples[:, cut:])  1.06 us
    pallas_call x1, Pallas kernels, body(): call(functools.partial(rest_kernel, cut), 'rest', shape(blocks * left + 8...  0.78 us
  transfers between devices with their start and end apart: 7, of which 2 were waited for; matrix products, arithmetic and copies ran while one was open for 5% of the time, Pallas kernels for 33%

profile of v1, /device:TPU:0, one launch (start us, length us, event | category | flops | bytes accessed | tf_op | source)
XLA Modules:
  0.0 19.4 jit_solution(5721975498692915786)
XLA Ops:
  0.0 0.5 %collective-permute-start.1 = (f32[2,64,8,128]{3,2,1,0:T(8,128)}, f32[2,64,8,128]{3,2,1,0:T(8,128)S(1)}, u32[]{:S(2)}, u32[]{:S(2)}) collective-permute-start(f32[2,64,8,128]{3,2,1,0:T(8,128)} %bitcast.8), channel_id=1, source_target_pairs={{0,2},{2,0},{4,6},{6,4},{8,10},{10,8},{12,14},{14,12},{16,18},{18,... | collective-permute-start | bytes 1572872 | tf_op jit(solution)/shard_map/ppermute | solution.py:44
  0.5 1.1 %fusion = (f32[2,32,8,128]{3,2,1,0:T(8,128)S(1)}, f32[2,32,8,128]{3,2,1,0:T(8,128)S(1)}) fusion(f32[2,64,8,128]{3,2,1,0:T(8,128)} %bitcast.9), kind=kLoop, calls=%fused_computation | loop fusion | bytes 1048576 | tf_op jit(solution)/shard_map/slice | solution.py:285
  1.5 0.1 collective-permute-start.2
  1.6 2.9 %collective-permute-start = (f32[2,32,8,128]{3,2,1,0:T(8,128)S(1)}, f32[2,32,8,128]{3,2,1,0:T(8,128)S(1)}, u32[]{:S(2)}, u32[]{:S(2)}) collective-permute-start(f32[2,32,8,128]{3,2,1,0:T(8,128)S(1)} %get-tuple-element.26.raw), channel_id=1, source_target_pairs={{0,1},{1,0},{2,3},{3,2},{4,5},{5,4},{6,7},{7,6},{8,9},{9,8},{10,11... | collective-permute-start | bytes 786440 | tf_op jit(solution)/shard_map/ppermute | solution.py:28
  4.6 0.8 %collective-permute-start.6 = (f32[2,32,8,128]{3,2,1,0:T(8,128)S(1)}, f32[2,32,8,128]{3,2,1,0:T(8,128)S(1)}, u32[]{:S(2)}, u32[]{:S(2)}) collective-permute-start(f32[2,32,8,128]{3,2,1,0:T(8,128)S(1)} %get-tuple-element.26.raw), channel_id=1, source_target_pairs={{0,2},{2,4},{4,0},{6,8},{8,10},{10,12},{12,6},{14,16},{16,18},{18,... | collective-permute-start | bytes 786440 | tf_op jit(solution)/shard_map/ppermute | solution.py:39
  5.4 0.0 copy-start.1
  5.4 0.7 %copy-done.1 = f32[2,1024]{1,0:T(2,128)S(1)} copy-done((f32[2,1024]{1,0:T(2,128)S(1)}, f32[2,1024]{1,0:T(2,128)}, u32[]{:S(2)}) %copy-start.1) | copy-done | bytes 8216
  6.1 1.5 %prepare.1 = (bf16[9,256,256]{2,1,0:T(8,128)(2,1)S(1)}, bf16[9,256,256]{2,1,0:T(8,128)(2,1)S(1)}, f32[256,256]{1,0:T(8,128)S(1)}, f32[256,256]{1,0:T(8,128)S(1)}) custom-call(f32[2,1024]{1,0:T(2,128)S(1)} %copy-done.1, f32[2,32,8,128]{3,2,1,0:T(8,128)S(1)} %get-tuple-element.26.raw, f32[2,32,8,128]{3,2,1,0:T(8,128)S(1)} %get-tuple-element.25.rest), custom_call_target="tpu_custom_call" | custom-call | flops 1000 | bytes 1000 | tf_op jit(solution)/shard_map/prepare/pallas_call | solution.py:291
  7.7 0.8 %collective-permute-done.2.odd = f32[2,32,8,128]{3,2,1,0:T(8,128)S(1)} collective-permute-done((f32[2,32,8,128]{3,2,1,0:T(8,128)S(1)}, f32[2,32,8,128]{3,2,1,0:T(8,128)S(1)}, u32[]{:S(2)}, u32[]{:S(2)}) %collective-permute-start.2) | collective-permute-done | bytes 262176 | tf_op jit(solution)/shard_map/ppermute | solution.py:39
  8.4 0.0 collective-permute-done.1.even
  8.5 0.8 %rest.1.after = f32[264,256]{1,0:T(8,128)S(1)} custom-call(f32[2,64,8,128]{3,2,1,0:T(8,128)S(1)} %collective-permute-done.1.even, f32[2,32,8,128]{3,2,1,0:T(8,128)S(1)} %collective-permute-done.2.odd, f32[256,256]{1,0:T(8,128)S(1)} %get-tuple-element.15.partial, bf16[9,256,256]{2,1,0:T(8,128)(2,1)S(1)} %get-tuple-element.16.th, ...), custom_call_target="tpu_custom_call" | custom-call | flops 1000 | bytes 1000 | tf_op jit(solution)/shard_map/rest/pallas_call | solution.py:300
  9.2 2.1 %collective-permute-start.4 = (f32[264,256]{1,0:T(8,128)S(1)}, f32[264,256]{1,0:T(8,128)S(1)}, u32[]{:S(2)}, u32[]{:S(2)}) collective-permute-start(f32[264,256]{1,0:T(8,128)S(1)} %rest.1.after), channel_id=1, source_target_pairs={{0,1},{1,0},{2,3},{3,2},{4,5},{5,4},{6,7},{7,6},{8,9},{9,8},{10,11... | collective-permute-start | bytes 811016 | tf_op jit(solution)/shard_map/ppermute | solution.py:28
  11.3 0.0 collective-permute-done.own.refs_0_
  11.3 0.0 copy-start
  11.3 0.0 copy-start.2
  11.3 1.1 %collective-permute-start.3 = (f32[256,256]{1,0:T(8,128)S(1)}, f32[256,256]{1,0:T(8,128)S(1)}, u32[]{:S(2)}, u32[]{:S(2)}) collective-permute-start(f32[256,256]{1,0:T(8,128)S(1)} %spill.2), channel_id=1, source_target_pairs={{0,2},{2,4},{4,0},{6,8},{8,10},{10,12},{12,6},{14,16},{16,18},{18,... | collective-permute-start | bytes 786440 | tf_op jit(solution)/shard_map/ppermute | solution.py:39
  12.4 0.7 %spill.3 = f32[256,256]{1,0:T(8,128)S(1)} custom-call(f32[2,32,8,128]{3,2,1,0:T(8,128)S(1)} %collective-permute-done.own.refs_0_, f32[264,256]{1,0:T(8,128)S(1)} %rest.1.after, bf16[9,256,256]{2,1,0:T(8,128)(2,1)S(1)} %get-tuple-element.16.th, bf16[9,256,256]{2,1,0:T(8,128)(2,1)S(1)} %get-tuple-element.17.tl), custom_call_target="tpu_custom_call" | custom-call | flops 1000 | bytes 1000 | tf_op jit(solution)/shard_map/spill/pallas_call | solution.py:311
  13.1 0.1 collective-permute-start.5
  13.2 0.0 collective-permute-done.6.odd
  13.2 0.0 copy-done
  13.2 0.0 copy-done.2
  13.2 3.3 %own.1 = (f32[2,128,8,2,128]{4,3,2,1,0:T(2,128)}, bf16[256,192]{1,0:T(8,128)(2,1)S(1)}, bf16[256,192]{1,0:T(8,128)(2,1)S(1)}, f32[256,256]{1,0:T(8,128)S(1)}) custom-call(s32[4,8]{1,0:T(4,128)S(1)} %bitcast.7, f32[16,2,8,32]{3,2,1,0:T(8,128)S(1)} %bitcast.6, f32[2,64,8,128]{3,2,1,0:T(8,128)S(1)} %collective-permute-done.1.even, ...), custom_call_target="tpu_custom_call" | custom-call | flops 1000 | bytes 1000 | tf_op jit(solution)/shard_map/own/pallas_call | solution.py:323
  16.6 1.1 %collective-permute-done.3.odd = f32[256,256]{1,0:T(8,128)S(1)} collective-permute-done((f32[256,256]{1,0:T(8,128)S(1)}, f32[256,256]{1,0:T(8,128)S(1)}, u32[]{:S(2)}, u32[]{:S(2)}) %collective-permute-start.3) | collective-permute-done | bytes 262176 | tf_op jit(solution)/shard_map/ppermute | solution.py:39
  17.7 0.0 collective-permute-done.4.rest
  17.7 0.1 ready.1.yb
  17.8 0.0 collective-permute-done.5.even
  17.8 1.6 %other.1 = f32[2,128,8,2,128]{4,3,2,1,0:T(2,128)} custom-call(bf16[192,1024]{1,0:T(8,128)(2,1)S(1)} %ready.1.yb, f32[256,256]{1,0:T(8,128)S(1)} %collective-permute-done.5.even, f32[256,256]{1,0:T(8,128)S(1)} %collective-permute-done.3.odd, f32[256,256]{1,0:T(8,128)S(1)} %get-tuple-element.21.partial, ...), custom_call_target="tpu_custom_call", output_to_operand_aliasing={{}: (6, {})} | custom-call | flops 1000 | bytes 1000 | tf_op jit(solution)/shard_map/other/pallas_call | solution.py:353
  (1 shorter events, 0.0 us)
Async XLA Ops:
  0.0 8.5 %collective-permute-start.1 = (f32[2,64,8,128]{3,2,1,0:T(8,128)}, f32[2,64,8,128]{3,2,1,0:T(8,128)S(1)}, u32[]{:S(2)}, u32[]{:S(2)}) collective-permute-start(f32[2,64,8,128]{3,2,1,0:T(8,128)} %bitcast.8), channel_id=1, source_target_pairs={{0,2},{2,0},{4,6},{6,4},{8,10},{10,8},{12,14},{14,12},{16,18},{18,... | collective-permute-start | bytes 1572872 | tf_op jit(solution)/shard_map/ppermute | solution.py:44
  1.5 6.9 %collective-permute-start.2 = (f32[2,32,8,128]{3,2,1,0:T(8,128)S(1)}, f32[2,32,8,128]{3,2,1,0:T(8,128)S(1)}, u32[]{:S(2)}, u32[]{:S(2)}) collective-permute-start(f32[2,32,8,128]{3,2,1,0:T(8,128)S(1)} %get-tuple-element.25.rest), channel_id=1, source_target_pairs={{0,2},{2,4},{4,0},{6,8},{8,10},{10,12},{12,6},{14,16},{16,18},{18,... | collective-permute-start | bytes 786440 | tf_op jit(solution)/shard_map/ppermute | solution.py:39
  1.6 9.7 %collective-permute-start = (f32[2,32,8,128]{3,2,1,0:T(8,128)S(1)}, f32[2,32,8,128]{3,2,1,0:T(8,128)S(1)}, u32[]{:S(2)}, u32[]{:S(2)}) collective-permute-start(f32[2,32,8,128]{3,2,1,0:T(8,128)S(1)} %get-tuple-element.26.raw), channel_id=1, source_target_pairs={{0,1},{1,0},{2,3},{3,2},{4,5},{5,4},{6,7},{7,6},{8,9},{9,8},{10,11... | collective-permute-start | bytes 786440 | tf_op jit(solution)/shard_map/ppermute | solution.py:28
  4.6 8.6 %collective-permute-start.6 = (f32[2,32,8,128]{3,2,1,0:T(8,128)S(1)}, f32[2,32,8,128]{3,2,1,0:T(8,128)S(1)}, u32[]{:S(2)}, u32[]{:S(2)}) collective-permute-start(f32[2,32,8,128]{3,2,1,0:T(8,128)S(1)} %get-tuple-element.26.raw), channel_id=1, source_target_pairs={{0,2},{2,4},{4,0},{6,8},{8,10},{10,12},{12,6},{14,16},{16,18},{18,... | collective-permute-start | bytes 786440 | tf_op jit(solution)/shard_map/ppermute | solution.py:39
  5.4 0.7 %copy-start.1 = (f32[2,1024]{1,0:T(2,128)S(1)}, f32[2,1024]{1,0:T(2,128)}, u32[]{:S(2)}) copy-start(f32[2,1024]{1,0:T(2,128)} %taps.1) | copy-start | bytes 24580
  9.2 8.5 %collective-permute-start.4 = (f32[264,256]{1,0:T(8,128)S(1)}, f32[264,256]{1,0:T(8,128)S(1)}, u32[]{:S(2)}, u32[]{:S(2)}) collective-permute-start(f32[264,256]{1,0:T(8,128)S(1)} %rest.1.after), channel_id=1, source_target_pairs={{0,1},{1,0},{2,3},{3,2},{4,5},{5,4},{6,7},{7,6},{8,9},{9,8},{10,11... | collective-permute-start | bytes 811016 | tf_op jit(solution)/shard_map/ppermute | solution.py:28
  11.3 1.9 %copy-start = (f32[16,2,32,8]{2,3,1,0:T(8,128)S(1)}, f32[16,2,32,8]{2,3,1,0:T(8,128)}, u32[]{:S(2)}) copy-start(f32[16,2,32,8]{2,3,1,0:T(8,128)} %param.5) | copy-start | bytes 98308
  11.3 1.9 %copy-start.2 = (s32[8,4]{0,1:T(4,128)S(1)}, s32[8,4]{0,1:T(4,128)}, u32[]{:S(2)}) copy-start(s32[8,4]{0,1:T(4,128)} %param.6) | copy-start | bytes 388
  11.3 6.4 %collective-permute-start.3 = (f32[256,256]{1,0:T(8,128)S(1)}, f32[256,256]{1,0:T(8,128)S(1)}, u32[]{:S(2)}, u32[]{:S(2)}) collective-permute-start(f32[256,256]{1,0:T(8,128)S(1)} %spill.2), channel_id=1, source_target_pairs={{0,2},{2,4},{4,0},{6,8},{8,10},{10,12},{12,6},{14,16},{16,18},{18,... | collective-permute-start | bytes 786440 | tf_op jit(solution)/shard_map/ppermute | solution.py:39
  13.1 4.7 %collective-permute-start.5 = (f32[256,256]{1,0:T(8,128)S(1)}, f32[256,256]{1,0:T(8,128)S(1)}, u32[]{:S(2)}, u32[]{:S(2)}) collective-permute-start(f32[256,256]{1,0:T(8,128)S(1)} %spill.3), channel_id=1, source_target_pairs={{0,2},{2,0},{4,6},{6,4},{8,10},{10,8},{12,14},{14,12},{16,18},{18,... | collective-permute-start | bytes 786440 | tf_op jit(solution)/shard_map/ppermute | solution.py:44

commit v2 on v1

--- a/solution.py
+++ b/solution.py
@@ -126,22 +126,31 @@
         out_ref[offset * rows :, :] += product(xh, xl, at, high_ref[offset], low_ref[offset])
 
 
-def spill(high_ref, low_ref, out_ref, xh, xl):
+def spill(high_ref, low_ref, out_ref, xh, xl, given=None):
     span = high_ref.shape[0] - 1
     rows = xh.shape[0] // span
-    for offset in range(1, span + 1):
+    whole = product(xh, xl, slice(0, span * rows), high_ref[span], low_ref[span])
+    out_ref[: span * rows, :] = whole if given is None else whole + given[: span * rows, :]
+    for offset in range(1, span):
         at = slice((span - offset) * rows, span * rows)
         out_ref[: offset * rows, :] += product(xh, xl, at, high_ref[offset], low_ref[offset])
 
 
-def outer(even_ref, start, odd_ref, high_ref, low_ref, out_ref, xh, xl):
-    rows, span = odd_ref.shape[1:3]
+def outer(even_ref, start, odd_ref, given, high_ref, low_ref, out_ref, xh, xl):
+    rows = odd_ref.shape[1]
     index = lax.axis_index("range")
-    odd = lax.rem(index, 2) == 1
-    for part in range(2):
-        value = jnp.where(odd, even_ref[part, start : start + rows], odd_ref[part])
-        place(jnp.swapaxes(jnp.where(index == 0, 0.0, value), 0, 1), xh, xl, part)
-    spill(high_ref, low_ref, out_ref, xh, xl)
+
+    @pl.when(index > 0)
+    def _():
+        for part in range(2):
+            value = even_ref[part, start : start + rows]
+            value = jnp.where(lax.rem(index, 2) == 1, value, odd_ref[part])
+            place(jnp.swapaxes(value, 0, 1), xh, xl, part)
+        spill(high_ref, low_ref, out_ref, xh, xl, given)
+
+    @pl.when(index == 0)
+    def _():
+        out_ref[...] = given[...]
 
 
 def columns(ref, y):
@@ -178,26 +187,22 @@
     return [(0, half), (half, blocks)] if half < blocks else [(0, blocks)]
 
 
-def prepare_kernel(taps, raw, rest, th, tl, raw_partial, rest_partial, *scratch):
+def prepare_kernel(taps, rest, th, tl, rest_partial, *scratch):
     make_tables(taps, th, tl)
     inner(rest, th, tl, rest_partial, *scratch[:2])
-    inner(raw, th, tl, raw_partial, *scratch[2:])
 
 
 def rest_kernel(cut, even, odd, partial, th, tl, out, xh, xl):
-    rows = partial.shape[0]
-    out[:rows, :] = partial[...]
-    out[rows:, :] = jnp.zeros((out.shape[0] - rows, out.shape[1]), f32)
-    outer(even, cut, odd, th, tl, out, xh, xl)
-
-
-def own_kernel(groups, others, plan, steer, even, odd, partial, rest, th, tl, *refs):
+    outer(even, cut, odd, partial, th, tl, out, xh, xl)
+
+
+def own_kernel(groups, others, plan, steer, even, odd, own, rest, th, tl, *refs):
     raws, (out, wa, wb), partials = refs[:others], refs[others : others + 3], refs[others + 3 : 2 * others + 3]
-    first, xh, xl, ya, yb, dense, sems, wide = refs[2 * others + 3 :]
+    whole, first, xh, xl, ya, yb, dense, sems, wide = refs[2 * others + 3 :]
     make_weights(plan, steer, (wa, wb), wide, groups)
     columns(rest, yb)
-    first[...] = partial[...]
-    outer(even, 0, odd, th, tl, first, xh, xl)
+    inner(own, th, tl, whole, xh, xl)
+    outer(even, 0, odd, whole, th, tl, first, xh, xl)
     columns(first, ya)
     copies = []
     for start, stop in parts_of(out.shape[2]):
@@ -217,15 +222,18 @@
     def _():
         for part in range(2):
             place(jnp.swapaxes(own[part, :, own.shape[2] - span :], 0, 1), xh, xl, part)
-        out[...] = jnp.zeros_like(out)
         spill(th, tl, out, xh, xl)
 
 
-def ready_kernel(odd, rest, yb):
+def ready_kernel(rest, yb):
     columns(rest, yb)
 
 
-def other_kernel(shift, yb, even, odd, partial, wa, wb, held, out, first, ya, dense, sems):
+def meet_kernel(odd, yb, token):
+    token[...] = jnp.zeros_like(token)
+
+
+def other_kernel(shift, yb, even, odd, partial, wa, wb, token, held, out, first, ya, dense, sems):
     index = lax.axis_index("range")
     count = even.shape[0]
     spilled = jnp.where(lax.rem(index, 2) == 1, even[...], odd[:count, :])
@@ -234,7 +242,7 @@
     first[:count, :] += spilled
     columns(first, ya)
     copies = []
-    for start, stop in parts_of(out.shape[2]):
+    for start, stop in [(0, out.shape[2])]:
         lanes = slice(start * TILE, stop * TILE)
         dense[:, lanes] = dot(wa[...], ya[:, lanes]) + dot(wb[...], yb[:, lanes])
         copies += send(shift, dense, out, start, stop, sems)
@@ -262,7 +270,7 @@
     subarrays, gates = echoes.shape[1], echoes.shape[3]
     blocks = gates // TILE
     span = filter_taps.shape[1] // TILE
-    assert echoes.shape[2] == 1 and blocks >= span and lax.axis_size("range") % 4 == 0
+    assert echoes.shape[2] == 1 and blocks == span and lax.axis_size("range") % 4 == 0
     cut = subarrays // 2
     left = subarrays - cut
     groups = ((0, cut), (cut, left))
@@ -288,19 +296,19 @@
     even = from_even(samples[:, :, tail])
     odd_raw = from_odd(raw[:, :, tail])
 
-    th, tl, raw_partial, rest_partial = call(
+    th, tl, rest_partial = call(
         prepare_kernel,
         "prepare",
         [shape(span + 1, 2 * TILE, 2 * TILE, dtype=bf16)] * 2
-        + [shape(blocks * rows, 2 * TILE) for rows in (cut, left)],
+        + [shape(blocks * left, 2 * TILE)],
+        [VMEM] * 2,
         [VMEM] * 3,
-        [VMEM] * 4,
-        [*halves(left), *halves(cut)],
-    )(filter_taps, raw, rest)
+        halves(left),
+    )(filter_taps, rest)
     own_rest = call(
         functools.partial(rest_kernel, cut),
         "rest",
-        shape(blocks * left + 8, 2 * TILE),
+        shape(blocks * left, 2 * TILE),
         [VMEM] * 5,
         VMEM,
         halves(left),
@@ -328,13 +336,13 @@
         + [shape(blocks * cut, 2 * TILE)] * others,
         [VMEM] * (8 + others),
         [any_space] + [VMEM] * (2 + others),
-        [first, *halves(cut), ya, yb, *dense, pltpu.VMEM((2 * subarrays, 2 * count), f32)],
+        [first, first, *halves(cut), ya, yb, *dense, pltpu.VMEM((2 * subarrays, 2 * count), f32)],
     )(
         plan.T,
         steer_blocks.transpose(0, 1, 3, 2),
         even,
         odd_raw,
-        raw_partial,
+        raw,
         own_rest,
         th,
         tl,
@@ -345,20 +353,23 @@
             ready_kernel,
             "ready",
             shape(6 * left, gates, dtype=bf16),
-            [any_space, VMEM],
+            [VMEM],
             VMEM,
             [],
-            flops=1 << 36,
-        )(odd_others[k - 1], others_rest[k - 1])
+            flops=1 << 30,
+        )(others_rest[k - 1])
+        token = call(
+            meet_kernel, "meet", shape(8, TILE), [any_space] * 2, VMEM, [], flops=1 << 36
+        )(odd_others[k - 1], ready)
         out = call(
             functools.partial(other_kernel, k),
             "other",
             out_shape,
-            [VMEM] * 6 + [any_space],
+            [VMEM] * 6 + [any_space] * 2,
             any_space,
             [first, ya, *dense],
-            input_output_aliases={6: 0},
-        )(ready, even_others[k - 1], odd_others[k - 1], partials[k - 1], wa, wb, out)
+            input_output_aliases={7: 0},
+        )(ready, even_others[k - 1], odd_others[k - 1], partials[k - 1], wa, wb, token, out)
     return out.transpose(0, 1, 3, 2, 4).reshape(2, count, pulses, gates)
 
 

time: 19.6 us -> 19.4 us (0.990)
  Pallas kernels: 8.04 us -> 6.31 us
  waiting for transfers between devices: 1.95 us -> 3.15 us
    ppermute x2, waiting for transfers between devices: 0.01 us -> 1.77 us  [shifted(): lax.ppermute(value, axis, [(i, (i + steps) % count) for i in range(count)])]
    pallas_call x2 -> x3, Pallas kernels: 0.85 us -> 0.09 us  [the longest x1 0.07 us: body(): call(ready_kernel, 'ready', shape(6 * left, gates, dtype=bf16), [VMEM], V...]
    ppermute x3, waiting for transfers between devices: 1.94 us -> 1.37 us  [from_odd(): return lax.ppermute(value, 'range', list(target.items()))]
    pallas_call x1, Pallas kernels: 1.53 us -> 1.02 us  [body(): call(prepare_kernel, 'prepare', [shape(span + 1, 2 * TILE, 2 * TILE, dtyp...]
    pallas_call x1, Pallas kernels: 3.34 us -> 2.9 us  [body(): call(functools.partial(own_kernel, groups, others), 'own', [out_shape] +...]
  transfers between devices with their start and end apart: 7 -> 7, of which waited for: 2 -> 4; matrix products, arithmetic and copies ran while one was open for 5% -> 6% of each run, Pallas kernels for 33% -> 25%
where the time goes in v2:
time: 19.4 us; the launch traced here: 19 us
  starting transfers between devices  7.75 us (40%)
  Pallas kernels  6.31 us (33%)
  waiting for transfers between devices  3.15 us (16%)
  local copies, waits for them, and re-layouts  1.77 us (9%)
    ppermute x2, starting transfers between devices, shifted(): lax.ppermute(value, axis, [(i, (i + steps) % count) for i in range(count)])  5 us
    pallas_call x1, Pallas kernels, body(): call(functools.partial(own_kernel, groups, others), 'own', [out_shape] +...  2.9 us
    ppermute x3, starting transfers between devices, from_odd(): return lax.ppermute(value, 'range', list(target.items()))  2.23 us
    ppermute x2, waiting for transfers between devices, shifted(): lax.ppermute(value, axis, [(i, (i + steps) % count) for i in range(count)])  1.77 us
    pallas_call x1, Pallas kernels, body(): call(functools.partial(other_kernel, k), 'other', out_shape, [VMEM] * 6 +...  1.55 us
    ppermute x3, waiting for transfers between devices, from_odd(): return lax.ppermute(value, 'range', list(target.items()))  1.37 us
    slice x1, local copies, waits for them, and re-layouts, body(): raw, rest = (samples[:, :cut], samples[:, cut:])  1.06 us
    pallas_call x1, Pallas kernels, body(): call(prepare_kernel, 'prepare', [shape(span + 1, 2 * TILE, 2 * TILE, dtyp...  1.02 us
  transfers between devices with their start and end apart: 7, of which 4 were waited for; matrix products, arithmetic and copies ran while one was open for 6% of the time, Pallas kernels for 25%

profile of v2, /device:TPU:0, one launch (start us, length us, event | category | flops | bytes accessed | tf_op | source)
XLA Modules:
  0.0 19.0 jit_solution(14214807730674170577)
XLA Ops:
  0.0 0.5 %collective-permute-start = (f32[2,64,8,128]{3,2,1,0:T(8,128)}, f32[2,64,8,128]{3,2,1,0:T(8,128)S(1)}, u32[]{:S(2)}, u32[]{:S(2)}) collective-permute-start(f32[2,64,8,128]{3,2,1,0:T(8,128)} %bitcast.8), channel_id=1, source_target_pairs={{0,2},{2,0},{4,6},{6,4},{8,10},{10,8},{12,14},{14,12},{16,18},{18,... | collective-permute-start | bytes 1572872 | tf_op jit(solution)/shard_map/ppermute | solution.py:44
  0.5 1.1 %fusion = (f32[2,32,8,128]{3,2,1,0:T(8,128)S(1)}, f32[2,32,8,128]{3,2,1,0:T(8,128)S(1)}) fusion(f32[2,64,8,128]{3,2,1,0:T(8,128)} %bitcast.9), kind=kLoop, calls=%fused_computation | loop fusion | bytes 1048576 | tf_op jit(solution)/shard_map/slice | solution.py:293
  1.5 0.1 collective-permute-start.1
  1.6 2.9 %collective-permute-start.3 = (f32[2,32,8,128]{3,2,1,0:T(8,128)S(1)}, f32[2,32,8,128]{3,2,1,0:T(8,128)S(1)}, u32[]{:S(2)}, u32[]{:S(2)}) collective-permute-start(f32[2,32,8,128]{3,2,1,0:T(8,128)S(1)} %get-tuple-element.23.own), channel_id=1, source_target_pairs={{0,1},{1,0},{2,3},{3,2},{4,5},{5,4},{6,7},{7,6},{8,9},{9,8},{10,11... | collective-permute-start | bytes 786440 | tf_op jit(solution)/shard_map/ppermute | solution.py:28
  4.6 0.8 %collective-permute-start.6 = (f32[2,32,8,128]{3,2,1,0:T(8,128)S(1)}, f32[2,32,8,128]{3,2,1,0:T(8,128)S(1)}, u32[]{:S(2)}, u32[]{:S(2)}) collective-permute-start(f32[2,32,8,128]{3,2,1,0:T(8,128)S(1)} %get-tuple-element.23.own), channel_id=1, source_target_pairs={{0,2},{2,4},{4,0},{6,8},{8,10},{10,12},{12,6},{14,16},{16,18},{18,... | collective-permute-start | bytes 786440 | tf_op jit(solution)/shard_map/ppermute | solution.py:39
  5.4 0.0 copy-start.1
  5.4 0.7 %copy-done.1 = f32[2,1024]{1,0:T(2,128)S(1)} copy-done((f32[2,1024]{1,0:T(2,128)S(1)}, f32[2,1024]{1,0:T(2,128)}, u32[]{:S(2)}) %copy-start.1) | copy-done | bytes 8216
  6.1 1.0 %prepare.1 = (bf16[9,256,256]{2,1,0:T(8,128)(2,1)S(1)}, bf16[9,256,256]{2,1,0:T(8,128)(2,1)S(1)}, f32[256,256]{1,0:T(8,128)S(1)}) custom-call(f32[2,1024]{1,0:T(2,128)S(1)} %copy-done.1, f32[2,32,8,128]{3,2,1,0:T(8,128)S(1)} %get-tuple-element.24.rest), custom_call_target="tpu_custom_call" | custom-call | flops 1000 | bytes 1000 | tf_op jit(solution)/shard_map/prepare/pallas_call | solution.py:299
  7.1 1.3 %collective-permute-done.1.odd = f32[2,32,8,128]{3,2,1,0:T(8,128)S(1)} collective-permute-done((f32[2,32,8,128]{3,2,1,0:T(8,128)S(1)}, f32[2,32,8,128]{3,2,1,0:T(8,128)S(1)}, u32[]{:S(2)}, u32[]{:S(2)}) %collective-permute-start.1) | collective-permute-done | bytes 262176 | tf_op jit(solution)/shard_map/ppermute | solution.py:39
  8.4 0.0 collective-permute-done.even
  8.5 2.1 %collective-permute-start.2 = (f32[256,256]{1,0:T(8,128)S(1)}, f32[256,256]{1,0:T(8,128)S(1)}, u32[]{:S(2)}, u32[]{:S(2)}) collective-permute-start(f32[256,256]{1,0:T(8,128)S(1)} %rest.1.after), channel_id=1, source_target_pairs={{0,1},{1,0},{2,3},{3,2},{4,5},{5,4},{6,7},{7,6},{8,9},{9,8},{10,11... | collective-permute-start | bytes 786440 | tf_op jit(solution)/shard_map/ppermute | solution.py:28
  10.5 0.6 %collective-permute-done.3.own.refs_0_ = f32[2,32,8,128]{3,2,1,0:T(8,128)S(1)} collective-permute-done((f32[2,32,8,128]{3,2,1,0:T(8,128)S(1)}, f32[2,32,8,128]{3,2,1,0:T(8,128)S(1)}, u32[]{:S(2)}, u32[]{:S(2)}) %collective-permute-start.3) | collective-permute-done | bytes 262176 | tf_op jit(solution)/shard_map/ppermute | solution.py:28
  11.1 0.0 copy-start
  11.1 0.0 copy-start.2
  11.1 1.3 %collective-permute-start.5 = (f32[256,256]{1,0:T(8,128)S(1)}, f32[256,256]{1,0:T(8,128)S(1)}, u32[]{:S(2)}, u32[]{:S(2)}) collective-permute-start(f32[256,256]{1,0:T(8,128)S(1)} %spill.3), channel_id=1, source_target_pairs={{0,2},{2,4},{4,0},{6,8},{8,10},{10,12},{12,6},{14,16},{16,18},{18,... | collective-permute-start | bytes 786440 | tf_op jit(solution)/shard_map/ppermute | solution.py:39
  12.4 0.7 %spill.2 = f32[256,256]{1,0:T(8,128)S(1)} custom-call(f32[2,32,8,128]{3,2,1,0:T(8,128)S(1)} %collective-permute-done.3.own.refs_0_, f32[256,256]{1,0:T(8,128)S(1)} %rest.1.after, bf16[9,256,256]{2,1,0:T(8,128)(2,1)S(1)} %get-tuple-element.15.th, bf16[9,256,256]{2,1,0:T(8,128)(2,1)S(1)} %get-tuple-element.16.tl), custom_call_target="tpu_custom_call" | custom-call | flops 1000 | bytes 1000 | tf_op jit(solution)/shard_map/spill/pallas_call | solution.py:319
  13.1 0.1 collective-permute-start.4
  13.2 0.0 collective-permute-done.6.odd
  13.2 0.0 copy-done
  13.2 0.0 copy-done.2
  13.3 2.9 %own.1 = (f32[2,128,8,2,128]{4,3,2,1,0:T(2,128)}, bf16[256,192]{1,0:T(8,128)(2,1)S(1)}, bf16[256,192]{1,0:T(8,128)(2,1)S(1)}, f32[256,256]{1,0:T(8,128)S(1)}) custom-call(s32[4,8]{1,0:T(4,128)S(1)} %bitcast.7, f32[16,2,8,32]{3,2,1,0:T(8,128)S(1)} %bitcast.6, f32[2,64,8,128]{3,2,1,0:T(8,128)S(1)} %collective-permute-done.even, ...), custom_call_target="tpu_custom_call" | custom-call | flops 1000 | bytes 1000 | tf_op jit(solution)/shard_map/own/pallas_call | solution.py:331
  16.2 1.2 %collective-permute-done.2.rest = f32[256,256]{1,0:T(8,128)S(1)} collective-permute-done((f32[256,256]{1,0:T(8,128)S(1)}, f32[256,256]{1,0:T(8,128)S(1)}, u32[]{:S(2)}, u32[]{:S(2)}) %collective-permute-start.2) | collective-permute-done | bytes 262176 | tf_op jit(solution)/shard_map/ppermute | solution.py:28
  17.4 0.1 ready.1.yb
  17.4 0.1 collective-permute-done.5.odd
  17.5 0.0 collective-permute-done.4.even
  17.5 1.5 %other.1 = f32[2,128,8,2,128]{4,3,2,1,0:T(2,128)} custom-call(bf16[192,1024]{1,0:T(8,128)(2,1)S(1)} %ready.1.yb, f32[256,256]{1,0:T(8,128)S(1)} %collective-permute-done.4.even, f32[256,256]{1,0:T(8,128)S(1)} %collective-permute-done.5.odd, f32[256,256]{1,0:T(8,128)S(1)} %get-tuple-element.19.partial, ...), custom_call_target="tpu_custom_call", output_to_operand_aliasing={{}: (7, {})} | custom-call | flops 1000 | bytes 1000 | tf_op jit(solution)/shard_map/other/pallas_call | solution.py:364
  (3 shorter events, 0.0 us)
Async XLA Ops:
  0.0 8.5 %collective-permute-start = (f32[2,64,8,128]{3,2,1,0:T(8,128)}, f32[2,64,8,128]{3,2,1,0:T(8,128)S(1)}, u32[]{:S(2)}, u32[]{:S(2)}) collective-permute-start(f32[2,64,8,128]{3,2,1,0:T(8,128)} %bitcast.8), channel_id=1, source_target_pairs={{0,2},{2,0},{4,6},{6,4},{8,10},{10,8},{12,14},{14,12},{16,18},{18,... | collective-permute-start | bytes 1572872 | tf_op jit(solution)/shard_map/ppermute | solution.py:44
  1.5 6.9 %collective-permute-start.1 = (f32[2,32,8,128]{3,2,1,0:T(8,128)S(1)}, f32[2,32,8,128]{3,2,1,0:T(8,128)S(1)}, u32[]{:S(2)}, u32[]{:S(2)}) collective-permute-start(f32[2,32,8,128]{3,2,1,0:T(8,128)S(1)} %get-tuple-element.24.rest), channel_id=1, source_target_pairs={{0,2},{2,4},{4,0},{6,8},{8,10},{10,12},{12,6},{14,16},{16,18},{18,... | collective-permute-start | bytes 786440 | tf_op jit(solution)/shard_map/ppermute | solution.py:39
  1.6 9.5 %collective-permute-start.3 = (f32[2,32,8,128]{3,2,1,0:T(8,128)S(1)}, f32[2,32,8,128]{3,2,1,0:T(8,128)S(1)}, u32[]{:S(2)}, u32[]{:S(2)}) collective-permute-start(f32[2,32,8,128]{3,2,1,0:T(8,128)S(1)} %get-tuple-element.23.own), channel_id=1, source_target_pairs={{0,1},{1,0},{2,3},{3,2},{4,5},{5,4},{6,7},{7,6},{8,9},{9,8},{10,11... | collective-permute-start | bytes 786440 | tf_op jit(solution)/shard_map/ppermute | solution.py:28
  4.6 8.6 %collective-permute-start.6 = (f32[2,32,8,128]{3,2,1,0:T(8,128)S(1)}, f32[2,32,8,128]{3,2,1,0:T(8,128)S(1)}, u32[]{:S(2)}, u32[]{:S(2)}) collective-permute-start(f32[2,32,8,128]{3,2,1,0:T(8,128)S(1)} %get-tuple-element.23.own), channel_id=1, source_target_pairs={{0,2},{2,4},{4,0},{6,8},{8,10},{10,12},{12,6},{14,16},{16,18},{18,... | collective-permute-start | bytes 786440 | tf_op jit(solution)/shard_map/ppermute | solution.py:39
  5.4 0.7 %copy-start.1 = (f32[2,1024]{1,0:T(2,128)S(1)}, f32[2,1024]{1,0:T(2,128)}, u32[]{:S(2)}) copy-start(f32[2,1024]{1,0:T(2,128)} %taps.1) | copy-start | bytes 24580
  8.5 8.9 %collective-permute-start.2 = (f32[256,256]{1,0:T(8,128)S(1)}, f32[256,256]{1,0:T(8,128)S(1)}, u32[]{:S(2)}, u32[]{:S(2)}) collective-permute-start(f32[256,256]{1,0:T(8,128)S(1)} %rest.1.after), channel_id=1, source_target_pairs={{0,1},{1,0},{2,3},{3,2},{4,5},{5,4},{6,7},{7,6},{8,9},{9,8},{10,11... | collective-permute-start | bytes 786440 | tf_op jit(solution)/shard_map/ppermute | solution.py:28
  11.1 2.1 %copy-start = (f32[16,2,32,8]{2,3,1,0:T(8,128)S(1)}, f32[16,2,32,8]{2,3,1,0:T(8,128)}, u32[]{:S(2)}) copy-start(f32[16,2,32,8]{2,3,1,0:T(8,128)} %param.5) | copy-start | bytes 98308
  11.1 2.1 %copy-start.2 = (s32[8,4]{0,1:T(4,128)S(1)}, s32[8,4]{0,1:T(4,128)}, u32[]{:S(2)}) copy-start(s32[8,4]{0,1:T(4,128)} %param.6) | copy-start | bytes 388
  11.1 6.4 %collective-permute-start.5 = (f32[256,256]{1,0:T(8,128)S(1)}, f32[256,256]{1,0:T(8,128)S(1)}, u32[]{:S(2)}, u32[]{:S(2)}) collective-permute-start(f32[256,256]{1,0:T(8,128)S(1)} %spill.3), channel_id=1, source_target_pairs={{0,2},{2,4},{4,0},{6,8},{8,10},{10,12},{12,6},{14,16},{16,18},{18,... | collective-permute-start | bytes 786440 | tf_op jit(solution)/shard_map/ppermute | solution.py:39
  13.1 4.4 %collective-permute-start.4 = (f32[256,256]{1,0:T(8,128)S(1)}, f32[256,256]{1,0:T(8,128)S(1)}, u32[]{:S(2)}, u32[]{:S(2)}) collective-permute-start(f32[256,256]{1,0:T(8,128)S(1)} %spill.2), channel_id=1, source_target_pairs={{0,2},{2,0},{4,6},{6,4},{8,10},{10,8},{12,14},{14,12},{16,18},{18,... | collective-permute-start | bytes 786440 | tf_op jit(solution)/shard_map/ppermute | solution.py:44

commit v3 on v2

--- a/solution.py
+++ b/solution.py
@@ -101,13 +101,12 @@
         ref[...] = jnp.concatenate([high, high, low], axis=1)
 
 
-def place(value, xh, xl, part):
-    blocks, rows = value.shape[:2]
-    for block in range(blocks):
-        high, low = split(value[block])
-        at = (slice(block * rows, (block + 1) * rows), slice(part * TILE, (part + 1) * TILE))
-        xh[at] = high
-        xl[at] = low
+def place(value, block, xh, xl, part):
+    rows = value.shape[0]
+    high, low = split(value)
+    at = (slice(block * rows, (block + 1) * rows), slice(part * TILE, (part + 1) * TILE))
+    xh[at] = high
+    xl[at] = low
 
 
 def product(xh, xl, at, high, low):
@@ -118,7 +117,9 @@
     rows, blocks = own_ref.shape[1:3]
     span = high_ref.shape[0] - 1
     for part in range(2):
-        place(jnp.swapaxes(own_ref[part], 0, 1), xh, xl, part)
+        value = jnp.swapaxes(own_ref[part], 0, 1)
+        for block in range(blocks):
+            place(value[block], block, xh, xl, part)
     at = slice(0, blocks * rows)
     out_ref[...] = product(xh, xl, at, high_ref[0], low_ref[0])
     for offset in range(1, min(span + 1, blocks)):
@@ -126,14 +127,29 @@
         out_ref[offset * rows :, :] += product(xh, xl, at, high_ref[offset], low_ref[offset])
 
 
-def spill(high_ref, low_ref, out_ref, xh, xl, given=None):
+def spill(values, high_ref, low_ref, out_ref, xh, both, given=None):
     span = high_ref.shape[0] - 1
     rows = xh.shape[0] // span
-    whole = product(xh, xl, slice(0, span * rows), high_ref[span], low_ref[span])
-    out_ref[: span * rows, :] = whole if given is None else whole + given[: span * rows, :]
-    for offset in range(1, span):
-        at = slice((span - offset) * rows, span * rows)
-        out_ref[: offset * rows, :] += product(xh, xl, at, high_ref[offset], low_ref[offset])
+    for offset in range(1, span + 1):
+        block = span - offset
+        for part in range(2):
+            high, low = split(values[part][block])
+            lanes = slice(part * TILE, (part + 1) * TILE)
+            xh[block * rows : (block + 1) * rows, lanes] = high
+            both[2 * block * rows : (2 * block + 1) * rows, lanes] = high
+            both[(2 * block + 1) * rows : (2 * block + 2) * rows, lanes] = low
+        pair = dot(both[2 * block * rows :, :], high_ref[offset])
+        rest = dot(xh[block * rows :, :], low_ref[offset])
+        for target in range(offset):
+            at = slice(target * rows, (target + 1) * rows)
+            term = pair[2 * target * rows : (2 * target + 1) * rows, :] + rest[at, :]
+            term = term + pair[(2 * target + 1) * rows : (2 * target + 2) * rows, :]
+            if target < offset - 1:
+                out_ref[at, :] += term
+            elif given is None:
+                out_ref[at, :] = term
+            else:
+                out_ref[at, :] = term + given[at, :]
 
 
 def outer(even_ref, start, odd_ref, given, high_ref, low_ref, out_ref, xh, xl):
@@ -142,11 +158,12 @@
 
     @pl.when(index > 0)
     def _():
+        values = []
         for part in range(2):
             value = even_ref[part, start : start + rows]
             value = jnp.where(lax.rem(index, 2) == 1, value, odd_ref[part])
-            place(jnp.swapaxes(value, 0, 1), xh, xl, part)
-        spill(high_ref, low_ref, out_ref, xh, xl, given)
+            values.append(jnp.swapaxes(value, 0, 1))
+        spill(values, high_ref, low_ref, out_ref, xh, xl, given)
 
     @pl.when(index == 0)
     def _():
@@ -198,11 +215,11 @@
 
 def own_kernel(groups, others, plan, steer, even, odd, own, rest, th, tl, *refs):
     raws, (out, wa, wb), partials = refs[:others], refs[others : others + 3], refs[others + 3 : 2 * others + 3]
-    whole, first, xh, xl, ya, yb, dense, sems, wide = refs[2 * others + 3 :]
+    whole, first, xh, xl, both, ya, yb, dense, sems, wide = refs[2 * others + 3 :]
     make_weights(plan, steer, (wa, wb), wide, groups)
     columns(rest, yb)
     inner(own, th, tl, whole, xh, xl)
-    outer(even, 0, odd, whole, th, tl, first, xh, xl)
+    outer(even, 0, odd, whole, th, tl, first, xh, both)
     columns(first, ya)
     copies = []
     for start, stop in parts_of(out.shape[2]):
@@ -220,9 +237,8 @@
 
     @pl.when(lax.rem(lax.axis_index("range"), 2) == parity)
     def _():
-        for part in range(2):
-            place(jnp.swapaxes(own[part, :, own.shape[2] - span :], 0, 1), xh, xl, part)
-        spill(th, tl, out, xh, xl)
+        values = [jnp.swapaxes(own[part, :, own.shape[2] - span :], 0, 1) for part in range(2)]
+        spill(values, th, tl, out, xh, xl)
 
 
 def ready_kernel(rest, yb):
@@ -283,6 +299,9 @@
     def halves(rows):
         return [pltpu.VMEM((blocks * rows, 2 * TILE), bf16)] * 2
 
+    def spilling(rows):
+        return [pltpu.VMEM((k * span * rows, 2 * TILE), bf16) for k in (1, 2)]
+
     out_shape = shape(2, count, blocks, pulses, TILE)
     ya, yb = (pltpu.VMEM((6 * rows, gates), bf16) for rows in (cut, left))
     first = pltpu.VMEM((blocks * cut, 2 * TILE), f32)
@@ -311,7 +330,7 @@
         shape(blocks * left, 2 * TILE),
         [VMEM] * 5,
         VMEM,
-        halves(left),
+        spilling(left),
     )(even, odd_rest, rest_partial, th, tl)
     others_rest = [shifted(own_rest, "pulse", k) for k in range(1, pulses)]
     others_raw, own_rest = lax.optimization_barrier((others_raw, own_rest))
@@ -322,7 +341,7 @@
             shape(span * cut + more, 2 * TILE),
             [VMEM, any_space, VMEM, VMEM],
             VMEM,
-            [pltpu.VMEM((span * cut, 2 * TILE), bf16)] * 2,
+            spilling(cut),
             flops=flops,
         )(raw, own_rest, th, tl)
 
@@ -336,7 +355,7 @@
         + [shape(blocks * cut, 2 * TILE)] * others,
         [VMEM] * (8 + others),
         [any_space] + [VMEM] * (2 + others),
-        [first, first, *halves(cut), ya, yb, *dense, pltpu.VMEM((2 * subarrays, 2 * count), f32)],
+        [first, first, *halves(cut), spilling(cut)[1], ya, yb, *dense, pltpu.VMEM((2 * subarrays, 2 * count), f32)],
     )(
         plan.T,
         steer_blocks.transpose(0, 1, 3, 2),

time: 19.4 us -> 19.4 us (level)
  no operation moved by 1% of the time
where the time goes in v3:
time: 19.4 us; the launch traced here: 19 us
  starting transfers between devices  7.68 us (40%)
  Pallas kernels  6.24 us (32%)
  waiting for transfers between devices  3.28 us (17%)
  local copies, waits for them, and re-layouts  1.77 us (9%)
    ppermute x2, starting transfers between devices, shifted(): lax.ppermute(value, axis, [(i, (i + steps) % count) for i in range(count)])  5 us
    pallas_call x1, Pallas kernels, body(): call(functools.partial(own_kernel, groups, others), 'own', [out_shape] +...  2.9 us
    ppermute x3, starting transfers between devices, from_odd(): return lax.ppermute(value, 'range', list(target.items()))  2.17 us
    ppermute x2, waiting for transfers between devices, shifted(): lax.ppermute(value, axis, [(i, (i + steps) % count) for i in range(count)])  1.91 us
    pallas_call x1, Pallas kernels, body(): call(functools.partial(other_kernel, k), 'other', out_shape, [VMEM] * 6 +...  1.55 us
    ppermute x3, waiting for transfers between devices, from_odd(): return lax.ppermute(value, 'range', list(target.items()))  1.37 us
    slice x1, local copies, waits for them, and re-layouts, body(): raw, rest = (samples[:, :cut], samples[:, cut:])  1.06 us
    pallas_call x1, Pallas kernels, body(): call(prepare_kernel, 'prepare', [shape(span + 1, 2 * TILE, 2 * TILE, dtyp...  1.02 us
  transfers between devices with their start and end apart: 7, of which 4 were waited for; matrix products, arithmetic and copies ran while one was open for 6% of the time, Pallas kernels for 25%

profile of v3, /device:TPU:0, one launch (start us, length us, event | category | flops | bytes accessed | tf_op | source)
XLA Modules:
  0.0 19.0 jit_solution(3362038897511469830)
XLA Ops:
  0.0 0.5 %collective-permute-start = (f32[2,64,8,128]{3,2,1,0:T(8,128)}, f32[2,64,8,128]{3,2,1,0:T(8,128)S(1)}, u32[]{:S(2)}, u32[]{:S(2)}) collective-permute-start(f32[2,64,8,128]{3,2,1,0:T(8,128)} %bitcast.8), channel_id=1, source_target_pairs={{0,2},{2,0},{4,6},{6,4},{8,10},{10,8},{12,14},{14,12},{16,18},{18,... | collective-permute-start | bytes 1572872 | tf_op jit(solution)/shard_map/ppermute | solution.py:44
  0.5 1.1 %fusion = (f32[2,32,8,128]{3,2,1,0:T(8,128)S(1)}, f32[2,32,8,128]{3,2,1,0:T(8,128)S(1)}) fusion(f32[2,64,8,128]{3,2,1,0:T(8,128)} %bitcast.9), kind=kLoop, calls=%fused_computation | loop fusion | bytes 1048576 | tf_op jit(solution)/shard_map/slice | solution.py:312
  1.5 0.1 collective-permute-start.1
  1.6 2.9 %collective-permute-start.3 = (f32[2,32,8,128]{3,2,1,0:T(8,128)S(1)}, f32[2,32,8,128]{3,2,1,0:T(8,128)S(1)}, u32[]{:S(2)}, u32[]{:S(2)}) collective-permute-start(f32[2,32,8,128]{3,2,1,0:T(8,128)S(1)} %get-tuple-element.23.own), channel_id=1, source_target_pairs={{0,1},{1,0},{2,3},{3,2},{4,5},{5,4},{6,7},{7,6},{8,9},{9,8},{10,11... | collective-permute-start | bytes 786440 | tf_op jit(solution)/shard_map/ppermute | solution.py:28
  4.6 0.8 %collective-permute-start.6 = (f32[2,32,8,128]{3,2,1,0:T(8,128)S(1)}, f32[2,32,8,128]{3,2,1,0:T(8,128)S(1)}, u32[]{:S(2)}, u32[]{:S(2)}) collective-permute-start(f32[2,32,8,128]{3,2,1,0:T(8,128)S(1)} %get-tuple-element.23.own), channel_id=1, source_target_pairs={{0,2},{2,4},{4,0},{6,8},{8,10},{10,12},{12,6},{14,16},{16,18},{18,... | collective-permute-start | bytes 786440 | tf_op jit(solution)/shard_map/ppermute | solution.py:39
  5.4 0.0 copy-start.1
  5.4 0.7 %copy-done.1 = f32[2,1024]{1,0:T(2,128)S(1)} copy-done((f32[2,1024]{1,0:T(2,128)S(1)}, f32[2,1024]{1,0:T(2,128)}, u32[]{:S(2)}) %copy-start.1) | copy-done | bytes 8216
  6.1 1.0 %prepare.1 = (bf16[9,256,256]{2,1,0:T(8,128)(2,1)S(1)}, bf16[9,256,256]{2,1,0:T(8,128)(2,1)S(1)}, f32[256,256]{1,0:T(8,128)S(1)}) custom-call(f32[2,1024]{1,0:T(2,128)S(1)} %copy-done.1, f32[2,32,8,128]{3,2,1,0:T(8,128)S(1)} %get-tuple-element.24.rest), custom_call_target="tpu_custom_call" | custom-call | flops 1000 | bytes 1000 | tf_op jit(solution)/shard_map/prepare/pallas_call | solution.py:318
  7.1 1.3 %collective-permute-done.1.odd = f32[2,32,8,128]{3,2,1,0:T(8,128)S(1)} collective-permute-done((f32[2,32,8,128]{3,2,1,0:T(8,128)S(1)}, f32[2,32,8,128]{3,2,1,0:T(8,128)S(1)}, u32[]{:S(2)}, u32[]{:S(2)}) %collective-permute-start.1) | collective-permute-done | bytes 262176 | tf_op jit(solution)/shard_map/ppermute | solution.py:39
  8.4 0.0 collective-permute-done.even
  8.5 2.1 %collective-permute-start.2 = (f32[256,256]{1,0:T(8,128)S(1)}, f32[256,256]{1,0:T(8,128)S(1)}, u32[]{:S(2)}, u32[]{:S(2)}) collective-permute-start(f32[256,256]{1,0:T(8,128)S(1)} %rest.1.after), channel_id=1, source_target_pairs={{0,1},{1,0},{2,3},{3,2},{4,5},{5,4},{6,7},{7,6},{8,9},{9,8},{10,11... | collective-permute-start | bytes 786440 | tf_op jit(solution)/shard_map/ppermute | solution.py:28
  10.5 0.6 %collective-permute-done.3.own.refs_0_ = f32[2,32,8,128]{3,2,1,0:T(8,128)S(1)} collective-permute-done((f32[2,32,8,128]{3,2,1,0:T(8,128)S(1)}, f32[2,32,8,128]{3,2,1,0:T(8,128)S(1)}, u32[]{:S(2)}, u32[]{:S(2)}) %collective-permute-start.3) | collective-permute-done | bytes 262176 | tf_op jit(solution)/shard_map/ppermute | solution.py:28
  11.1 0.0 copy-start
  11.1 0.0 copy-start.2
  11.1 1.2 %collective-permute-start.5 = (f32[256,256]{1,0:T(8,128)S(1)}, f32[256,256]{1,0:T(8,128)S(1)}, u32[]{:S(2)}, u32[]{:S(2)}) collective-permute-start(f32[256,256]{1,0:T(8,128)S(1)} %spill.3), channel_id=1, source_target_pairs={{0,2},{2,4},{4,0},{6,8},{8,10},{10,12},{12,6},{14,16},{16,18},{18,... | collective-permute-start | bytes 786440 | tf_op jit(solution)/shard_map/ppermute | solution.py:39
  12.3 0.7 %spill.2 = f32[256,256]{1,0:T(8,128)S(1)} custom-call(f32[2,32,8,128]{3,2,1,0:T(8,128)S(1)} %collective-permute-done.3.own.refs_0_, f32[256,256]{1,0:T(8,128)S(1)} %rest.1.after, bf16[9,256,256]{2,1,0:T(8,128)(2,1)S(1)} %get-tuple-element.15.th, bf16[9,256,256]{2,1,0:T(8,128)(2,1)S(1)} %get-tuple-element.16.tl), custom_call_target="tpu_custom_call" | custom-call | flops 1000 | bytes 1000 | tf_op jit(solution)/shard_map/spill/pallas_call | solution.py:338
  13.0 0.1 collective-permute-start.4
  13.1 0.0 collective-permute-done.6.odd
  13.1 0.0 copy-done
  13.1 0.0 copy-done.2
  13.1 2.9 %own.1 = (f32[2,128,8,2,128]{4,3,2,1,0:T(2,128)}, bf16[256,192]{1,0:T(8,128)(2,1)S(1)}, bf16[256,192]{1,0:T(8,128)(2,1)S(1)}, f32[256,256]{1,0:T(8,128)S(1)}) custom-call(s32[4,8]{1,0:T(4,128)S(1)} %bitcast.7, f32[16,2,8,32]{3,2,1,0:T(8,128)S(1)} %bitcast.6, f32[2,64,8,128]{3,2,1,0:T(8,128)S(1)} %collective-permute-done.even, ...), custom_call_target="tpu_custom_call" | custom-call | flops 1000 | bytes 1000 | tf_op jit(solution)/shard_map/own/pallas_call | solution.py:350
  16.0 1.3 %collective-permute-done.2.rest = f32[256,256]{1,0:T(8,128)S(1)} collective-permute-done((f32[256,256]{1,0:T(8,128)S(1)}, f32[256,256]{1,0:T(8,128)S(1)}, u32[]{:S(2)}, u32[]{:S(2)}) %collective-permute-start.2) | collective-permute-done | bytes 262176 | tf_op jit(solution)/shard_map/ppermute | solution.py:28
  17.4 0.1 ready.1.yb
  17.4 0.1 collective-permute-done.5.odd
  17.5 0.0 collective-permute-done.4.even
  17.5 1.5 %other.1 = f32[2,128,8,2,128]{4,3,2,1,0:T(2,128)} custom-call(bf16[192,1024]{1,0:T(8,128)(2,1)S(1)} %ready.1.yb, f32[256,256]{1,0:T(8,128)S(1)} %collective-permute-done.4.even, f32[256,256]{1,0:T(8,128)S(1)} %collective-permute-done.5.odd, f32[256,256]{1,0:T(8,128)S(1)} %get-tuple-element.19.partial, ...), custom_call_target="tpu_custom_call", output_to_operand_aliasing={{}: (7, {})} | custom-call | flops 1000 | bytes 1000 | tf_op jit(solution)/shard_map/other/pallas_call | solution.py:383
  (3 shorter events, 0.0 us)
Async XLA Ops:
  0.0 8.5 %collective-permute-start = (f32[2,64,8,128]{3,2,1,0:T(8,128)}, f32[2,64,8,128]{3,2,1,0:T(8,128)S(1)}, u32[]{:S(2)}, u32[]{:S(2)}) collective-permute-start(f32[2,64,8,128]{3,2,1,0:T(8,128)} %bitcast.8), channel_id=1, source_target_pairs={{0,2},{2,0},{4,6},{6,4},{8,10},{10,8},{12,14},{14,12},{16,18},{18,... | collective-permute-start | bytes 1572872 | tf_op jit(solution)/shard_map/ppermute | solution.py:44
  1.5 6.9 %collective-permute-start.1 = (f32[2,32,8,128]{3,2,1,0:T(8,128)S(1)}, f32[2,32,8,128]{3,2,1,0:T(8,128)S(1)}, u32[]{:S(2)}, u32[]{:S(2)}) collective-permute-start(f32[2,32,8,128]{3,2,1,0:T(8,128)S(1)} %get-tuple-element.24.rest), channel_id=1, source_target_pairs={{0,2},{2,4},{4,0},{6,8},{8,10},{10,12},{12,6},{14,16},{16,18},{18,... | collective-permute-start | bytes 786440 | tf_op jit(solution)/shard_map/ppermute | solution.py:39
  1.6 9.5 %collective-permute-start.3 = (f32[2,32,8,128]{3,2,1,0:T(8,128)S(1)}, f32[2,32,8,128]{3,2,1,0:T(8,128)S(1)}, u32[]{:S(2)}, u32[]{:S(2)}) collective-permute-start(f32[2,32,8,128]{3,2,1,0:T(8,128)S(1)} %get-tuple-element.23.own), channel_id=1, source_target_pairs={{0,1},{1,0},{2,3},{3,2},{4,5},{5,4},{6,7},{7,6},{8,9},{9,8},{10,11... | collective-permute-start | bytes 786440 | tf_op jit(solution)/shard_map/ppermute | solution.py:28
  4.6 8.5 %collective-permute-start.6 = (f32[2,32,8,128]{3,2,1,0:T(8,128)S(1)}, f32[2,32,8,128]{3,2,1,0:T(8,128)S(1)}, u32[]{:S(2)}, u32[]{:S(2)}) collective-permute-start(f32[2,32,8,128]{3,2,1,0:T(8,128)S(1)} %get-tuple-element.23.own), channel_id=1, source_target_pairs={{0,2},{2,4},{4,0},{6,8},{8,10},{10,12},{12,6},{14,16},{16,18},{18,... | collective-permute-start | bytes 786440 | tf_op jit(solution)/shard_map/ppermute | solution.py:39
  5.4 0.7 %copy-start.1 = (f32[2,1024]{1,0:T(2,128)S(1)}, f32[2,1024]{1,0:T(2,128)}, u32[]{:S(2)}) copy-start(f32[2,1024]{1,0:T(2,128)} %taps.1) | copy-start | bytes 24580
  8.5 8.9 %collective-permute-start.2 = (f32[256,256]{1,0:T(8,128)S(1)}, f32[256,256]{1,0:T(8,128)S(1)}, u32[]{:S(2)}, u32[]{:S(2)}) collective-permute-start(f32[256,256]{1,0:T(8,128)S(1)} %rest.1.after), channel_id=1, source_target_pairs={{0,1},{1,0},{2,3},{3,2},{4,5},{5,4},{6,7},{7,6},{8,9},{9,8},{10,11... | collective-permute-start | bytes 786440 | tf_op jit(solution)/shard_map/ppermute | solution.py:28
  11.1 2.0 %copy-start = (f32[16,2,32,8]{2,3,1,0:T(8,128)S(1)}, f32[16,2,32,8]{2,3,1,0:T(8,128)}, u32[]{:S(2)}) copy-start(f32[16,2,32,8]{2,3,1,0:T(8,128)} %param.5) | copy-start | bytes 98308
  11.1 2.0 %copy-start.2 = (s32[8,4]{0,1:T(4,128)S(1)}, s32[8,4]{0,1:T(4,128)}, u32[]{:S(2)}) copy-start(s32[8,4]{0,1:T(4,128)} %param.6) | copy-start | bytes 388
  11.1 6.4 %collective-permute-start.5 = (f32[256,256]{1,0:T(8,128)S(1)}, f32[256,256]{1,0:T(8,128)S(1)}, u32[]{:S(2)}, u32[]{:S(2)}) collective-permute-start(f32[256,256]{1,0:T(8,128)S(1)} %spill.3), channel_id=1, source_target_pairs={{0,2},{2,4},{4,0},{6,8},{8,10},{10,12},{12,6},{14,16},{16,18},{18,... | collective-permute-start | bytes 786440 | tf_op jit(solution)/shard_map/ppermute | solution.py:39
  13.0 4.5 %collective-permute-start.4 = (f32[256,256]{1,0:T(8,128)S(1)}, f32[256,256]{1,0:T(8,128)S(1)}, u32[]{:S(2)}, u32[]{:S(2)}) collective-permute-start(f32[256,256]{1,0:T(8,128)S(1)} %spill.2), channel_id=1, source_target_pairs={{0,2},{2,0},{4,6},{6,4},{8,10},{10,8},{12,14},{14,12},{16,18},{18,... | collective-permute-start | bytes 786440 | tf_op jit(solution)/shard_map/ppermute | solution.py:44

commit v4 on v3

--- a/solution.py
+++ b/solution.py
@@ -183,19 +183,17 @@
 
 
 def send(shift, dense, out_ref, start, stop, sems):
-    count = dense.shape[0] // 2
-    pulses = out_ref.shape[3]
+    pulses = out_ref.shape[2]
     pulse = lax.rem(lax.axis_index("pulse") + pulses - shift, pulses)
     copies = []
     for block in range(start, stop):
-        for part in range(2):
-            copy = pltpu.make_async_copy(
-                dense.at[part * count : (part + 1) * count, block * TILE : (block + 1) * TILE],
-                out_ref.at[part, :, block, pulse, :],
-                sems.at[2 * block + part],
-            )
-            copy.start()
-            copies.append(copy)
+        copy = pltpu.make_async_copy(
+            dense.at[:, block * TILE : (block + 1) * TILE],
+            out_ref.at[:, block, pulse, :],
+            sems.at[block],
+        )
+        copy.start()
+        copies.append(copy)
     return copies
 
 
@@ -222,7 +220,7 @@
     outer(even, 0, odd, whole, th, tl, first, xh, both)
     columns(first, ya)
     copies = []
-    for start, stop in parts_of(out.shape[2]):
+    for start, stop in parts_of(out.shape[1]):
         lanes = slice(start * TILE, stop * TILE)
         dense[:, lanes] = dot(wa[...], ya[:, lanes]) + dot(wb[...], yb[:, lanes])
         copies += send(0, dense, out, start, stop, sems)
@@ -258,7 +256,7 @@
     first[:count, :] += spilled
     columns(first, ya)
     copies = []
-    for start, stop in [(0, out.shape[2])]:
+    for start, stop in [(0, out.shape[1])]:
         lanes = slice(start * TILE, stop * TILE)
         dense[:, lanes] = dot(wa[...], ya[:, lanes]) + dot(wb[...], yb[:, lanes])
         copies += send(shift, dense, out, start, stop, sems)
@@ -302,10 +300,10 @@
     def spilling(rows):
         return [pltpu.VMEM((k * span * rows, 2 * TILE), bf16) for k in (1, 2)]
 
-    out_shape = shape(2, count, blocks, pulses, TILE)
+    out_shape = shape(2 * count, blocks, pulses, TILE)
     ya, yb = (pltpu.VMEM((6 * rows, gates), bf16) for rows in (cut, left))
     first = pltpu.VMEM((blocks * cut, 2 * TILE), f32)
-    dense = [pltpu.VMEM((2 * count, gates), f32), pltpu.SemaphoreType.DMA((2 * blocks,))]
+    dense = [pltpu.VMEM((2 * count, gates), f32), pltpu.SemaphoreType.DMA((blocks,))]
 
     samples = echoes.reshape(2, subarrays, blocks, TILE)
     tail = slice(blocks - span, blocks)
@@ -389,7 +387,7 @@
             [first, ya, *dense],
             input_output_aliases={7: 0},
         )(ready, even_others[k - 1], odd_others[k - 1], partials[k - 1], wa, wb, token, out)
-    return out.transpose(0, 1, 3, 2, 4).reshape(2, count, pulses, gates)
+    return out.transpose(0, 2, 1, 3).reshape(2, count, pulses, gates)
 
 
 def solution(mesh):

time: 19.4 us -> 19.3 us (level)
  transfers between devices with their start and end apart: 7 -> 7, of which waited for: 4 -> 4; matrix products, arithmetic and copies ran while one was open for 6% -> 6% of each run, Pallas kernels for 25% -> 24%
where the time goes in v4:
time: 19.3 us; the launch traced here: 19 us
  starting transfers between devices  7.68 us (40%)
  Pallas kernels  6.06 us (31%)
  waiting for transfers between devices  3.4 us (18%)
  local copies, waits for them, and re-layouts  1.77 us (9%)
    ppermute x2, starting transfers between devices, shifted(): lax.ppermute(value, axis, [(i, (i + steps) % count) for i in range(count)])  5 us
    pallas_call x1, Pallas kernels, body(): call(functools.partial(own_kernel, groups, others), 'own', [out_shape] +...  2.78 us
    ppermute x3, starting transfers between devices, from_odd(): return lax.ppermute(value, 'range', list(target.items()))  2.17 us
    ppermute x2, waiting for transfers between devices, shifted(): lax.ppermute(value, axis, [(i, (i + steps) % count) for i in range(count)])  2.03 us
    pallas_call x1, Pallas kernels, body(): call(functools.partial(other_kernel, k), 'other', out_shape, [VMEM] * 6 +...  1.48 us
    ppermute x3, waiting for transfers between devices, from_odd(): return lax.ppermute(value, 'range', list(target.items()))  1.37 us
    slice x1, local copies, waits for them, and re-layouts, body(): raw, rest = (samples[:, :cut], samples[:, cut:])  1.06 us
    pallas_call x1, Pallas kernels, body(): call(prepare_kernel, 'prepare', [shape(span + 1, 2 * TILE, 2 * TILE, dtyp...  1.02 us
  transfers between devices with their start and end apart: 7, of which 4 were waited for; matrix products, arithmetic and copies ran while one was open for 6% of the time, Pallas kernels for 24%

profile of v4, /device:TPU:0, one launch (start us, length us, event | category | flops | bytes accessed | tf_op | source)
XLA Modules:
  0.0 19.0 jit_solution(6632438852754299675)
XLA Ops:
  0.0 0.5 %collective-permute-start = (f32[2,64,8,128]{3,2,1,0:T(8,128)}, f32[2,64,8,128]{3,2,1,0:T(8,128)S(1)}, u32[]{:S(2)}, u32[]{:S(2)}) collective-permute-start(f32[2,64,8,128]{3,2,1,0:T(8,128)} %bitcast.8), channel_id=1, source_target_pairs={{0,2},{2,0},{4,6},{6,4},{8,10},{10,8},{12,14},{14,12},{16,18},{18,... | collective-permute-start | bytes 1572872 | tf_op jit(solution)/shard_map/ppermute | solution.py:44
  0.5 1.1 %fusion = (f32[2,32,8,128]{3,2,1,0:T(8,128)S(1)}, f32[2,32,8,128]{3,2,1,0:T(8,128)S(1)}) fusion(f32[2,64,8,128]{3,2,1,0:T(8,128)} %bitcast.9), kind=kLoop, calls=%fused_computation | loop fusion | bytes 1048576 | tf_op jit(solution)/shard_map/slice | solution.py:310
  1.5 0.1 collective-permute-start.1
  1.6 2.9 %collective-permute-start.3 = (f32[2,32,8,128]{3,2,1,0:T(8,128)S(1)}, f32[2,32,8,128]{3,2,1,0:T(8,128)S(1)}, u32[]{:S(2)}, u32[]{:S(2)}) collective-permute-start(f32[2,32,8,128]{3,2,1,0:T(8,128)S(1)} %get-tuple-element.23.own), channel_id=1, source_target_pairs={{0,1},{1,0},{2,3},{3,2},{4,5},{5,4},{6,7},{7,6},{8,9},{9,8},{10,11... | collective-permute-start | bytes 786440 | tf_op jit(solution)/shard_map/ppermute | solution.py:28
  4.6 0.8 %collective-permute-start.6 = (f32[2,32,8,128]{3,2,1,0:T(8,128)S(1)}, f32[2,32,8,128]{3,2,1,0:T(8,128)S(1)}, u32[]{:S(2)}, u32[]{:S(2)}) collective-permute-start(f32[2,32,8,128]{3,2,1,0:T(8,128)S(1)} %get-tuple-element.23.own), channel_id=1, source_target_pairs={{0,2},{2,4},{4,0},{6,8},{8,10},{10,12},{12,6},{14,16},{16,18},{18,... | collective-permute-start | bytes 786440 | tf_op jit(solution)/shard_map/ppermute | solution.py:39
  5.4 0.0 copy-start.1
  5.4 0.7 %copy-done.1 = f32[2,1024]{1,0:T(2,128)S(1)} copy-done((f32[2,1024]{1,0:T(2,128)S(1)}, f32[2,1024]{1,0:T(2,128)}, u32[]{:S(2)}) %copy-start.1) | copy-done | bytes 8216
  6.1 1.0 %prepare.1 = (bf16[9,256,256]{2,1,0:T(8,128)(2,1)S(1)}, bf16[9,256,256]{2,1,0:T(8,128)(2,1)S(1)}, f32[256,256]{1,0:T(8,128)S(1)}) custom-call(f32[2,1024]{1,0:T(2,128)S(1)} %copy-done.1, f32[2,32,8,128]{3,2,1,0:T(8,128)S(1)} %get-tuple-element.24.rest), custom_call_target="tpu_custom_call" | custom-call | flops 1000 | bytes 1000 | tf_op jit(solution)/shard_map/prepare/pallas_call | solution.py:316
  7.1 1.3 %collective-permute-done.1.odd = f32[2,32,8,128]{3,2,1,0:T(8,128)S(1)} collective-permute-done((f32[2,32,8,128]{3,2,1,0:T(8,128)S(1)}, f32[2,32,8,128]{3,2,1,0:T(8,128)S(1)}, u32[]{:S(2)}, u32[]{:S(2)}) %collective-permute-start.1) | collective-permute-done | bytes 262176 | tf_op jit(solution)/shard_map/ppermute | solution.py:39
  8.4 0.0 collective-permute-done.even
  8.5 2.1 %collective-permute-start.2 = (f32[256,256]{1,0:T(8,128)S(1)}, f32[256,256]{1,0:T(8,128)S(1)}, u32[]{:S(2)}, u32[]{:S(2)}) collective-permute-start(f32[256,256]{1,0:T(8,128)S(1)} %rest.1.after), channel_id=1, source_target_pairs={{0,1},{1,0},{2,3},{3,2},{4,5},{5,4},{6,7},{7,6},{8,9},{9,8},{10,11... | collective-permute-start | bytes 786440 | tf_op jit(solution)/shard_map/ppermute | solution.py:28
  10.5 0.6 %collective-permute-done.3.own.refs_0_ = f32[2,32,8,128]{3,2,1,0:T(8,128)S(1)} collective-permute-done((f32[2,32,8,128]{3,2,1,0:T(8,128)S(1)}, f32[2,32,8,128]{3,2,1,0:T(8,128)S(1)}, u32[]{:S(2)}, u32[]{:S(2)}) %collective-permute-start.3) | collective-permute-done | bytes 262176 | tf_op jit(solution)/shard_map/ppermute | solution.py:28
  11.1 0.0 copy-start
  11.1 0.0 copy-start.2
  11.1 1.2 %collective-permute-start.5 = (f32[256,256]{1,0:T(8,128)S(1)}, f32[256,256]{1,0:T(8,128)S(1)}, u32[]{:S(2)}, u32[]{:S(2)}) collective-permute-start(f32[256,256]{1,0:T(8,128)S(1)} %spill.3), channel_id=1, source_target_pairs={{0,2},{2,4},{4,0},{6,8},{8,10},{10,12},{12,6},{14,16},{16,18},{18,... | collective-permute-start | bytes 786440 | tf_op jit(solution)/shard_map/ppermute | solution.py:39
  12.3 0.7 %spill.2 = f32[256,256]{1,0:T(8,128)S(1)} custom-call(f32[2,32,8,128]{3,2,1,0:T(8,128)S(1)} %collective-permute-done.3.own.refs_0_, f32[256,256]{1,0:T(8,128)S(1)} %rest.1.after, bf16[9,256,256]{2,1,0:T(8,128)(2,1)S(1)} %get-tuple-element.15.th, bf16[9,256,256]{2,1,0:T(8,128)(2,1)S(1)} %get-tuple-element.16.tl), custom_call_target="tpu_custom_call" | custom-call | flops 1000 | bytes 1000 | tf_op jit(solution)/shard_map/spill/pallas_call | solution.py:336
  13.0 0.1 collective-permute-start.4
  13.1 0.0 collective-permute-done.6.odd
  13.1 0.0 copy-done
  13.1 0.0 copy-done.2
  13.1 2.8 %own.1 = (f32[256,8,2,128]{3,2,1,0:T(2,128)}, bf16[256,192]{1,0:T(8,128)(2,1)S(1)}, bf16[256,192]{1,0:T(8,128)(2,1)S(1)}, f32[256,256]{1,0:T(8,128)S(1)}) custom-call(s32[4,8]{1,0:T(4,128)S(1)} %bitcast.7, f32[16,2,8,32]{3,2,1,0:T(8,128)S(1)} %bitcast.6, f32[2,64,8,128]{3,2,1,0:T(8,128)S(1)} %collective-permute-done.even, ...), custom_call_target="tpu_custom_call" | custom-call | flops 1000 | bytes 1000 | tf_op jit(solution)/shard_map/own/pallas_call | solution.py:348
  15.9 1.4 %collective-permute-done.2.rest = f32[256,256]{1,0:T(8,128)S(1)} collective-permute-done((f32[256,256]{1,0:T(8,128)S(1)}, f32[256,256]{1,0:T(8,128)S(1)}, u32[]{:S(2)}, u32[]{:S(2)}) %collective-permute-start.2) | collective-permute-done | bytes 262176 | tf_op jit(solution)/shard_map/ppermute | solution.py:28
  17.4 0.1 ready.1.yb
  17.4 0.1 collective-permute-done.5.odd
  17.5 0.0 collective-permute-done.4.even
  17.5 1.5 %other.1 = f32[256,8,2,128]{3,2,1,0:T(2,128)} custom-call(bf16[192,1024]{1,0:T(8,128)(2,1)S(1)} %ready.1.yb, f32[256,256]{1,0:T(8,128)S(1)} %collective-permute-done.4.even, f32[256,256]{1,0:T(8,128)S(1)} %collective-permute-done.5.odd, f32[256,256]{1,0:T(8,128)S(1)} %get-tuple-element.19.partial, ...), custom_call_target="tpu_custom_call", output_to_operand_aliasing={{}: (7, {})} | custom-call | flops 1000 | bytes 1000 | tf_op jit(solution)/shard_map/other/pallas_call | solution.py:381
  (3 shorter events, 0.0 us)
Async XLA Ops:
  0.0 8.5 %collective-permute-start = (f32[2,64,8,128]{3,2,1,0:T(8,128)}, f32[2,64,8,128]{3,2,1,0:T(8,128)S(1)}, u32[]{:S(2)}, u32[]{:S(2)}) collective-permute-start(f32[2,64,8,128]{3,2,1,0:T(8,128)} %bitcast.8), channel_id=1, source_target_pairs={{0,2},{2,0},{4,6},{6,4},{8,10},{10,8},{12,14},{14,12},{16,18},{18,... | collective-permute-start | bytes 1572872 | tf_op jit(solution)/shard_map/ppermute | solution.py:44
  1.5 6.9 %collective-permute-start.1 = (f32[2,32,8,128]{3,2,1,0:T(8,128)S(1)}, f32[2,32,8,128]{3,2,1,0:T(8,128)S(1)}, u32[]{:S(2)}, u32[]{:S(2)}) collective-permute-start(f32[2,32,8,128]{3,2,1,0:T(8,128)S(1)} %get-tuple-element.24.rest), channel_id=1, source_target_pairs={{0,2},{2,4},{4,0},{6,8},{8,10},{10,12},{12,6},{14,16},{16,18},{18,... | collective-permute-start | bytes 786440 | tf_op jit(solution)/shard_map/ppermute | solution.py:39
  1.6 9.5 %collective-permute-start.3 = (f32[2,32,8,128]{3,2,1,0:T(8,128)S(1)}, f32[2,32,8,128]{3,2,1,0:T(8,128)S(1)}, u32[]{:S(2)}, u32[]{:S(2)}) collective-permute-start(f32[2,32,8,128]{3,2,1,0:T(8,128)S(1)} %get-tuple-element.23.own), channel_id=1, source_target_pairs={{0,1},{1,0},{2,3},{3,2},{4,5},{5,4},{6,7},{7,6},{8,9},{9,8},{10,11... | collective-permute-start | bytes 786440 | tf_op jit(solution)/shard_map/ppermute | solution.py:28
  4.6 8.5 %collective-permute-start.6 = (f32[2,32,8,128]{3,2,1,0:T(8,128)S(1)}, f32[2,32,8,128]{3,2,1,0:T(8,128)S(1)}, u32[]{:S(2)}, u32[]{:S(2)}) collective-permute-start(f32[2,32,8,128]{3,2,1,0:T(8,128)S(1)} %get-tuple-element.23.own), channel_id=1, source_target_pairs={{0,2},{2,4},{4,0},{6,8},{8,10},{10,12},{12,6},{14,16},{16,18},{18,... | collective-permute-start | bytes 786440 | tf_op jit(solution)/shard_map/ppermute | solution.py:39
  5.4 0.7 %copy-start.1 = (f32[2,1024]{1,0:T(2,128)S(1)}, f32[2,1024]{1,0:T(2,128)}, u32[]{:S(2)}) copy-start(f32[2,1024]{1,0:T(2,128)} %taps.1) | copy-start | bytes 24580
  8.5 8.9 %collective-permute-start.2 = (f32[256,256]{1,0:T(8,128)S(1)}, f32[256,256]{1,0:T(8,128)S(1)}, u32[]{:S(2)}, u32[]{:S(2)}) collective-permute-start(f32[256,256]{1,0:T(8,128)S(1)} %rest.1.after), channel_id=1, source_target_pairs={{0,1},{1,0},{2,3},{3,2},{4,5},{5,4},{6,7},{7,6},{8,9},{9,8},{10,11... | collective-permute-start | bytes 786440 | tf_op jit(solution)/shard_map/ppermute | solution.py:28
  11.1 2.0 %copy-start = (f32[16,2,32,8]{2,3,1,0:T(8,128)S(1)}, f32[16,2,32,8]{2,3,1,0:T(8,128)}, u32[]{:S(2)}) copy-start(f32[16,2,32,8]{2,3,1,0:T(8,128)} %param.5) | copy-start | bytes 98308
  11.1 2.0 %copy-start.2 = (s32[8,4]{0,1:T(4,128)S(1)}, s32[8,4]{0,1:T(4,128)}, u32[]{:S(2)}) copy-start(s32[8,4]{0,1:T(4,128)} %param.6) | copy-start | bytes 388
  11.1 6.4 %collective-permute-start.5 = (f32[256,256]{1,0:T(8,128)S(1)}, f32[256,256]{1,0:T(8,128)S(1)}, u32[]{:S(2)}, u32[]{:S(2)}) collective-permute-start(f32[256,256]{1,0:T(8,128)S(1)} %spill.3), channel_id=1, source_target_pairs={{0,2},{2,4},{4,0},{6,8},{8,10},{10,12},{12,6},{14,16},{16,18},{18,... | collective-permute-start | bytes 786440 | tf_op jit(solution)/shard_map/ppermute | solution.py:39
  13.0 4.5 %collective-permute-start.4 = (f32[256,256]{1,0:T(8,128)S(1)}, f32[256,256]{1,0:T(8,128)S(1)}, u32[]{:S(2)}, u32[]{:S(2)}) collective-permute-start(f32[256,256]{1,0:T(8,128)S(1)} %spill.2), channel_id=1, source_target_pairs={{0,2},{2,0},{4,6},{6,4},{8,10},{10,8},{12,14},{14,12},{16,18},{18,... | collective-permute-start | bytes 786440 | tf_op jit(solution)/shard_map/ppermute | solution.py:44

commit v5 on v4

--- a/solution.py
+++ b/solution.py
@@ -11,7 +11,7 @@
 f32 = jnp.float32
 bf16 = jnp.bfloat16
 VMEM = pl.BlockSpec(memory_space=pltpu.VMEM)
-SMEM = pl.BlockSpec(memory_space=pltpu.SMEM)
+SHORT, LONG = 1000, 1 << 36
 
 
 def dot(left, right):
@@ -170,13 +170,15 @@
         out_ref[...] = given[...]
 
 
-def columns(ref, y):
+def columns(ref, y, added=None):
     blocks = y.shape[1] // TILE
     rows = y.shape[0] // 6
     for block in range(blocks):
         lanes = slice(block * TILE, (block + 1) * TILE)
+        at = slice(block * rows, (block + 1) * rows)
+        total = ref[at, :] if added is None else ref[at, :] + added[at, :]
         for part in range(2):
-            high, low = split(ref[block * rows : (block + 1) * rows, part * TILE : (part + 1) * TILE])
+            high, low = split(total[:, part * TILE : (part + 1) * TILE])
             for copy, value in enumerate((high, low, high)):
                 base = (2 * copy + part) * rows
                 y[base : base + rows, lanes] = value
@@ -202,9 +204,9 @@
     return [(0, half), (half, blocks)] if half < blocks else [(0, blocks)]
 
 
-def prepare_kernel(taps, rest, th, tl, rest_partial, *scratch):
+def prepare_kernel(taps, rest, th, tl, partial, xh, xl):
     make_tables(taps, th, tl)
-    inner(rest, th, tl, rest_partial, *scratch[:2])
+    inner(rest, th, tl, partial, xh, xl)
 
 
 def rest_kernel(cut, even, odd, partial, th, tl, out, xh, xl):
@@ -247,24 +249,16 @@
     token[...] = jnp.zeros_like(token)
 
 
-def other_kernel(shift, yb, even, odd, partial, wa, wb, token, held, out, first, ya, dense, sems):
+def other_kernel(shift, yb, even, odd, partial, wa, wb, token, held, out, ya, dense, sems):
     index = lax.axis_index("range")
-    count = even.shape[0]
-    spilled = jnp.where(lax.rem(index, 2) == 1, even[...], odd[:count, :])
-    spilled = jnp.where(index == 0, 0.0, spilled)
-    first[...] = partial[...]
-    first[:count, :] += spilled
-    columns(first, ya)
-    copies = []
-    for start, stop in [(0, out.shape[1])]:
-        lanes = slice(start * TILE, stop * TILE)
-        dense[:, lanes] = dot(wa[...], ya[:, lanes]) + dot(wb[...], yb[:, lanes])
-        copies += send(shift, dense, out, start, stop, sems)
-    for copy in copies:
+    spilled = jnp.where(lax.rem(index, 2) == 1, even[...], odd[...])
+    columns(partial, ya, jnp.where(index == 0, 0.0, spilled))
+    dense[...] = dot(wa[...], ya[...]) + dot(wb[...], yb[...])
+    for copy in send(shift, dense, out, 0, out.shape[1], sems):
         copy.wait()
 
 
-def call(kernel, name, out_shape, in_specs, out_specs, scratch_shapes, flops=1000, **kwargs):
+def call(kernel, name, out_shape, in_specs, out_specs, scratch_shapes, flops=SHORT, **kwargs):
     return pl.pallas_call(
         kernel,
         out_shape=out_shape,
@@ -306,12 +300,11 @@
     dense = [pltpu.VMEM((2 * count, gates), f32), pltpu.SemaphoreType.DMA((blocks,))]
 
     samples = echoes.reshape(2, subarrays, blocks, TILE)
-    tail = slice(blocks - span, blocks)
     raw, rest = samples[:, :cut], samples[:, cut:]
-    odd_rest = from_odd(rest[:, :, tail])
+    odd_rest = from_odd(rest)
     others_raw = [shifted(raw, "pulse", k) for k in range(1, pulses)]
-    even = from_even(samples[:, :, tail])
-    odd_raw = from_odd(raw[:, :, tail])
+    even = from_even(samples)
+    odd_raw = from_odd(raw)
 
     th, tl, rest_partial = call(
         prepare_kernel,
@@ -332,19 +325,20 @@
     )(even, odd_rest, rest_partial, th, tl)
     others_rest = [shifted(own_rest, "pulse", k) for k in range(1, pulses)]
     others_raw, own_rest = lax.optimization_barrier((others_raw, own_rest))
-    def spilled(parity, raw, flops, more):
+
+    def spilled(parity, raw, flops):
         return call(
             functools.partial(spill_kernel, parity),
             "spill",
-            shape(span * cut + more, 2 * TILE),
+            shape(span * cut, 2 * TILE),
             [VMEM, any_space, VMEM, VMEM],
             VMEM,
             spilling(cut),
             flops=flops,
         )(raw, own_rest, th, tl)
 
-    odd_others = [from_odd(spilled(1, raw, 1 << 36, 0)) for raw in others_raw]
-    even_others = [from_even(spilled(0, raw, 1000, 0)) for raw in others_raw]
+    odd_others = [from_odd(spilled(1, raw, LONG)) for raw in others_raw]
+    even_others = [from_even(spilled(0, raw, SHORT)) for raw in others_raw]
     out, wa, wb, *partials = call(
         functools.partial(own_kernel, groups, others),
         "own",
@@ -353,7 +347,15 @@
         + [shape(blocks * cut, 2 * TILE)] * others,
         [VMEM] * (8 + others),
         [any_space] + [VMEM] * (2 + others),
-        [first, first, *halves(cut), spilling(cut)[1], ya, yb, *dense, pltpu.VMEM((2 * subarrays, 2 * count), f32)],
+        [
+            *[first] * 2,
+            *halves(cut),
+            spilling(cut)[1],
+            ya,
+            yb,
+            *dense,
+            pltpu.VMEM((2 * subarrays, 2 * count), f32),
+        ],
     )(
         plan.T,
         steer_blocks.transpose(0, 1, 3, 2),
@@ -373,10 +375,10 @@
             [VMEM],
             VMEM,
             [],
-            flops=1 << 30,
+            flops=LONG >> 6,
         )(others_rest[k - 1])
         token = call(
-            meet_kernel, "meet", shape(8, TILE), [any_space] * 2, VMEM, [], flops=1 << 36
+            meet_kernel, "meet", shape(8, TILE), [any_space] * 2, VMEM, [], flops=LONG
         )(odd_others[k - 1], ready)
         out = call(
             functools.partial(other_kernel, k),
@@ -384,7 +386,7 @@
             out_shape,
             [VMEM] * 6 + [any_space] * 2,
             any_space,
-            [first, ya, *dense],
+            [ya, *dense],
             input_output_aliases={7: 0},
         )(ready, even_others[k - 1], odd_others[k - 1], partials[k - 1], wa, wb, token, out)
     return out.transpose(0, 2, 1, 3).reshape(2, count, pulses, gates)

time: 19.3 us -> 19.3 us (level)
  no operation moved by 1% of the time
where the time goes in v5:
time: 19.3 us; the launch traced here: 19 us
  starting transfers between devices  7.68 us (40%)
  Pallas kernels  6.05 us (31%)
  waiting for transfers between devices  3.4 us (18%)
  local copies, waits for them, and re-layouts  1.77 us (9%)
    ppermute x2, starting transfers between devices, shifted(): lax.ppermute(value, axis, [(i, (i + steps) % count) for i in range(count)])  5 us
    pallas_call x1, Pallas kernels, body(): call(functools.partial(own_kernel, groups, others), 'own', [out_shape] +...  2.78 us
    ppermute x3, starting transfers between devices, from_odd(): return lax.ppermute(value, 'range', list(target.items()))  2.17 us
    ppermute x2, waiting for transfers between devices, shifted(): lax.ppermute(value, axis, [(i, (i + steps) % count) for i in range(count)])  2.03 us
    pallas_call x1, Pallas kernels, body(): call(functools.partial(other_kernel, k), 'other', out_shape, [VMEM] * 6 +...  1.48 us
    ppermute x3, waiting for transfers between devices, from_odd(): return lax.ppermute(value, 'range', list(target.items()))  1.37 us
    slice x1, local copies, waits for them, and re-layouts, body(): raw, rest = (samples[:, :cut], samples[:, cut:])  1.06 us
    pallas_call x1, Pallas kernels, body(): call(prepare_kernel, 'prepare', [shape(span + 1, 2 * TILE, 2 * TILE, dtyp...  1.02 us
  transfers between devices with their start and end apart: 7, of which 4 were waited for; matrix products, arithmetic and copies ran while one was open for 6% of the time, Pallas kernels for 24%

profile of v5, /device:TPU:0, one launch (start us, length us, event | category | flops | bytes accessed | tf_op | source)
XLA Modules:
  0.0 19.0 jit_solution(17279813985645671508)
XLA Ops:
  0.0 0.5 %collective-permute-start = (f32[2,64,8,128]{3,2,1,0:T(8,128)}, f32[2,64,8,128]{3,2,1,0:T(8,128)S(1)}, u32[]{:S(2)}, u32[]{:S(2)}) collective-permute-start(f32[2,64,8,128]{3,2,1,0:T(8,128)} %bitcast.8), channel_id=1, source_target_pairs={{0,2},{2,0},{4,6},{6,4},{8,10},{10,8},{12,14},{14,12},{16,18},{18,... | collective-permute-start | bytes 1572872 | tf_op jit(solution)/shard_map/ppermute | solution.py:44
  0.5 1.1 %fusion = (f32[2,32,8,128]{3,2,1,0:T(8,128)S(1)}, f32[2,32,8,128]{3,2,1,0:T(8,128)S(1)}) fusion(f32[2,64,8,128]{3,2,1,0:T(8,128)} %bitcast.9), kind=kLoop, calls=%fused_computation | loop fusion | bytes 1048576 | tf_op jit(solution)/shard_map/slice | solution.py:303
  1.5 0.1 collective-permute-start.1
  1.6 2.9 %collective-permute-start.3 = (f32[2,32,8,128]{3,2,1,0:T(8,128)S(1)}, f32[2,32,8,128]{3,2,1,0:T(8,128)S(1)}, u32[]{:S(2)}, u32[]{:S(2)}) collective-permute-start(f32[2,32,8,128]{3,2,1,0:T(8,128)S(1)} %get-tuple-element.23.own), channel_id=1, source_target_pairs={{0,1},{1,0},{2,3},{3,2},{4,5},{5,4},{6,7},{7,6},{8,9},{9,8},{10,11... | collective-permute-start | bytes 786440 | tf_op jit(solution)/shard_map/ppermute | solution.py:28
  4.6 0.8 %collective-permute-start.6 = (f32[2,32,8,128]{3,2,1,0:T(8,128)S(1)}, f32[2,32,8,128]{3,2,1,0:T(8,128)S(1)}, u32[]{:S(2)}, u32[]{:S(2)}) collective-permute-start(f32[2,32,8,128]{3,2,1,0:T(8,128)S(1)} %get-tuple-element.23.own), channel_id=1, source_target_pairs={{0,2},{2,4},{4,0},{6,8},{8,10},{10,12},{12,6},{14,16},{16,18},{18,... | collective-permute-start | bytes 786440 | tf_op jit(solution)/shard_map/ppermute | solution.py:39
  5.4 0.0 copy-start.1
  5.4 0.7 %copy-done.1 = f32[2,1024]{1,0:T(2,128)S(1)} copy-done((f32[2,1024]{1,0:T(2,128)S(1)}, f32[2,1024]{1,0:T(2,128)}, u32[]{:S(2)}) %copy-start.1) | copy-done | bytes 8216
  6.1 1.0 %prepare.1 = (bf16[9,256,256]{2,1,0:T(8,128)(2,1)S(1)}, bf16[9,256,256]{2,1,0:T(8,128)(2,1)S(1)}, f32[256,256]{1,0:T(8,128)S(1)}) custom-call(f32[2,1024]{1,0:T(2,128)S(1)} %copy-done.1, f32[2,32,8,128]{3,2,1,0:T(8,128)S(1)} %get-tuple-element.24.rest), custom_call_target="tpu_custom_call" | custom-call | flops 1000 | bytes 1000 | tf_op jit(solution)/shard_map/prepare/pallas_call | solution.py:309
  7.1 1.3 %collective-permute-done.1.odd = f32[2,32,8,128]{3,2,1,0:T(8,128)S(1)} collective-permute-done((f32[2,32,8,128]{3,2,1,0:T(8,128)S(1)}, f32[2,32,8,128]{3,2,1,0:T(8,128)S(1)}, u32[]{:S(2)}, u32[]{:S(2)}) %collective-permute-start.1) | collective-permute-done | bytes 262176 | tf_op jit(solution)/shard_map/ppermute | solution.py:39
  8.4 0.0 collective-permute-done.even
  8.5 2.1 %collective-permute-start.2 = (f32[256,256]{1,0:T(8,128)S(1)}, f32[256,256]{1,0:T(8,128)S(1)}, u32[]{:S(2)}, u32[]{:S(2)}) collective-permute-start(f32[256,256]{1,0:T(8,128)S(1)} %rest.1.after), channel_id=1, source_target_pairs={{0,1},{1,0},{2,3},{3,2},{4,5},{5,4},{6,7},{7,6},{8,9},{9,8},{10,11... | collective-permute-start | bytes 786440 | tf_op jit(solution)/shard_map/ppermute | solution.py:28
  10.5 0.6 %collective-permute-done.3.own.refs_0_ = f32[2,32,8,128]{3,2,1,0:T(8,128)S(1)} collective-permute-done((f32[2,32,8,128]{3,2,1,0:T(8,128)S(1)}, f32[2,32,8,128]{3,2,1,0:T(8,128)S(1)}, u32[]{:S(2)}, u32[]{:S(2)}) %collective-permute-start.3) | collective-permute-done | bytes 262176 | tf_op jit(solution)/shard_map/ppermute | solution.py:28
  11.1 0.0 copy-start
  11.1 0.0 copy-start.2
  11.1 1.2 %collective-permute-start.5 = (f32[256,256]{1,0:T(8,128)S(1)}, f32[256,256]{1,0:T(8,128)S(1)}, u32[]{:S(2)}, u32[]{:S(2)}) collective-permute-start(f32[256,256]{1,0:T(8,128)S(1)} %spill.3), channel_id=1, source_target_pairs={{0,2},{2,4},{4,0},{6,8},{8,10},{10,12},{12,6},{14,16},{16,18},{18,... | collective-permute-start | bytes 786440 | tf_op jit(solution)/shard_map/ppermute | solution.py:39
  12.3 0.7 %spill.2 = f32[256,256]{1,0:T(8,128)S(1)} custom-call(f32[2,32,8,128]{3,2,1,0:T(8,128)S(1)} %collective-permute-done.3.own.refs_0_, f32[256,256]{1,0:T(8,128)S(1)} %rest.1.after, bf16[9,256,256]{2,1,0:T(8,128)(2,1)S(1)} %get-tuple-element.15.th, bf16[9,256,256]{2,1,0:T(8,128)(2,1)S(1)} %get-tuple-element.16.tl), custom_call_target="tpu_custom_call" | custom-call | flops 1000 | bytes 1000 | tf_op jit(solution)/shard_map/spill/pallas_call | solution.py:330
  13.0 0.1 collective-permute-start.4
  13.1 0.0 collective-permute-done.6.odd
  13.1 0.0 copy-done
  13.1 0.0 copy-done.2
  13.1 2.8 %own.1 = (f32[256,8,2,128]{3,2,1,0:T(2,128)}, bf16[256,192]{1,0:T(8,128)(2,1)S(1)}, bf16[256,192]{1,0:T(8,128)(2,1)S(1)}, f32[256,256]{1,0:T(8,128)S(1)}) custom-call(s32[4,8]{1,0:T(4,128)S(1)} %bitcast.7, f32[16,2,8,32]{3,2,1,0:T(8,128)S(1)} %bitcast.6, f32[2,64,8,128]{3,2,1,0:T(8,128)S(1)} %collective-permute-done.even, ...), custom_call_target="tpu_custom_call" | custom-call | flops 1000 | bytes 1000 | tf_op jit(solution)/shard_map/own/pallas_call | solution.py:342
  15.9 1.4 %collective-permute-done.2.rest = f32[256,256]{1,0:T(8,128)S(1)} collective-permute-done((f32[256,256]{1,0:T(8,128)S(1)}, f32[256,256]{1,0:T(8,128)S(1)}, u32[]{:S(2)}, u32[]{:S(2)}) %collective-permute-start.2) | collective-permute-done | bytes 262176 | tf_op jit(solution)/shard_map/ppermute | solution.py:28
  17.4 0.1 ready.1.yb
  17.4 0.1 collective-permute-done.5.odd
  17.5 0.0 collective-permute-done.4.even
  17.5 1.5 %other.1 = f32[256,8,2,128]{3,2,1,0:T(2,128)} custom-call(bf16[192,1024]{1,0:T(8,128)(2,1)S(1)} %ready.1.yb, f32[256,256]{1,0:T(8,128)S(1)} %collective-permute-done.4.even, f32[256,256]{1,0:T(8,128)S(1)} %collective-permute-done.5.odd, f32[256,256]{1,0:T(8,128)S(1)} %get-tuple-element.19.partial, ...), custom_call_target="tpu_custom_call", output_to_operand_aliasing={{}: (7, {})} | custom-call | flops 1000 | bytes 1000 | tf_op jit(solution)/shard_map/other/pallas_call | solution.py:383
  (3 shorter events, 0.0 us)
Async XLA Ops:
  0.0 8.5 %collective-permute-start = (f32[2,64,8,128]{3,2,1,0:T(8,128)}, f32[2,64,8,128]{3,2,1,0:T(8,128)S(1)}, u32[]{:S(2)}, u32[]{:S(2)}) collective-permute-start(f32[2,64,8,128]{3,2,1,0:T(8,128)} %bitcast.8), channel_id=1, source_target_pairs={{0,2},{2,0},{4,6},{6,4},{8,10},{10,8},{12,14},{14,12},{16,18},{18,... | collective-permute-start | bytes 1572872 | tf_op jit(solution)/shard_map/ppermute | solution.py:44
  1.5 6.9 %collective-permute-start.1 = (f32[2,32,8,128]{3,2,1,0:T(8,128)S(1)}, f32[2,32,8,128]{3,2,1,0:T(8,128)S(1)}, u32[]{:S(2)}, u32[]{:S(2)}) collective-permute-start(f32[2,32,8,128]{3,2,1,0:T(8,128)S(1)} %get-tuple-element.24.rest), channel_id=1, source_target_pairs={{0,2},{2,4},{4,0},{6,8},{8,10},{10,12},{12,6},{14,16},{16,18},{18,... | collective-permute-start | bytes 786440 | tf_op jit(solution)/shard_map/ppermute | solution.py:39
  1.6 9.5 %collective-permute-start.3 = (f32[2,32,8,128]{3,2,1,0:T(8,128)S(1)}, f32[2,32,8,128]{3,2,1,0:T(8,128)S(1)}, u32[]{:S(2)}, u32[]{:S(2)}) collective-permute-start(f32[2,32,8,128]{3,2,1,0:T(8,128)S(1)} %get-tuple-element.23.own), channel_id=1, source_target_pairs={{0,1},{1,0},{2,3},{3,2},{4,5},{5,4},{6,7},{7,6},{8,9},{9,8},{10,11... | collective-permute-start | bytes 786440 | tf_op jit(solution)/shard_map/ppermute | solution.py:28
  4.6 8.5 %collective-permute-start.6 = (f32[2,32,8,128]{3,2,1,0:T(8,128)S(1)}, f32[2,32,8,128]{3,2,1,0:T(8,128)S(1)}, u32[]{:S(2)}, u32[]{:S(2)}) collective-permute-start(f32[2,32,8,128]{3,2,1,0:T(8,128)S(1)} %get-tuple-element.23.own), channel_id=1, source_target_pairs={{0,2},{2,4},{4,0},{6,8},{8,10},{10,12},{12,6},{14,16},{16,18},{18,... | collective-permute-start | bytes 786440 | tf_op jit(solution)/shard_map/ppermute | solution.py:39
  5.4 0.7 %copy-start.1 = (f32[2,1024]{1,0:T(2,128)S(1)}, f32[2,1024]{1,0:T(2,128)}, u32[]{:S(2)}) copy-start(f32[2,1024]{1,0:T(2,128)} %taps.1) | copy-start | bytes 24580
  8.5 8.9 %collective-permute-start.2 = (f32[256,256]{1,0:T(8,128)S(1)}, f32[256,256]{1,0:T(8,128)S(1)}, u32[]{:S(2)}, u32[]{:S(2)}) collective-permute-start(f32[256,256]{1,0:T(8,128)S(1)} %rest.1.after), channel_id=1, source_target_pairs={{0,1},{1,0},{2,3},{3,2},{4,5},{5,4},{6,7},{7,6},{8,9},{9,8},{10,11... | collective-permute-start | bytes 786440 | tf_op jit(solution)/shard_map/ppermute | solution.py:28
  11.1 2.0 %copy-start = (f32[16,2,32,8]{2,3,1,0:T(8,128)S(1)}, f32[16,2,32,8]{2,3,1,0:T(8,128)}, u32[]{:S(2)}) copy-start(f32[16,2,32,8]{2,3,1,0:T(8,128)} %param.5) | copy-start | bytes 98308
  11.1 2.0 %copy-start.2 = (s32[8,4]{0,1:T(4,128)S(1)}, s32[8,4]{0,1:T(4,128)}, u32[]{:S(2)}) copy-start(s32[8,4]{0,1:T(4,128)} %param.6) | copy-start | bytes 388
  11.1 6.4 %collective-permute-start.5 = (f32[256,256]{1,0:T(8,128)S(1)}, f32[256,256]{1,0:T(8,128)S(1)}, u32[]{:S(2)}, u32[]{:S(2)}) collective-permute-start(f32[256,256]{1,0:T(8,128)S(1)} %spill.3), channel_id=1, source_target_pairs={{0,2},{2,4},{4,0},{6,8},{8,10},{10,12},{12,6},{14,16},{16,18},{18,... | collective-permute-start | bytes 786440 | tf_op jit(solution)/shard_map/ppermute | solution.py:39
  13.0 4.5 %collective-permute-start.4 = (f32[256,256]{1,0:T(8,128)S(1)}, f32[256,256]{1,0:T(8,128)S(1)}, u32[]{:S(2)}, u32[]{:S(2)}) collective-permute-start(f32[256,256]{1,0:T(8,128)S(1)} %spill.2), channel_id=1, source_target_pairs={{0,2},{2,0},{4,6},{6,4},{8,10},{10,8},{12,14},{14,12},{16,18},{18,... | collective-permute-start | bytes 786440 | tf_op jit(solution)/shard_map/ppermute | solution.py:44

commit v6 on v5

--- a/solution.py
+++ b/solution.py
@@ -241,19 +241,20 @@
         spill(values, th, tl, out, xh, xl)
 
 
-def ready_kernel(rest, yb):
+def ready_kernel(rest, wb, out, yb):
     columns(rest, yb)
+    out[...] = dot(wb[...], yb[...])
 
 
 def meet_kernel(odd, yb, token):
     token[...] = jnp.zeros_like(token)
 
 
-def other_kernel(shift, yb, even, odd, partial, wa, wb, token, held, out, ya, dense, sems):
+def other_kernel(shift, part, even, odd, partial, wa, token, held, out, ya, dense, sems):
     index = lax.axis_index("range")
     spilled = jnp.where(lax.rem(index, 2) == 1, even[...], odd[...])
     columns(partial, ya, jnp.where(index == 0, 0.0, spilled))
-    dense[...] = dot(wa[...], ya[...]) + dot(wb[...], yb[...])
+    dense[...] = dot(wa[...], ya[...]) + part[...]
     for copy in send(shift, dense, out, 0, out.shape[1], sems):
         copy.wait()
 
@@ -371,12 +372,12 @@
         ready = call(
             ready_kernel,
             "ready",
-            shape(6 * left, gates, dtype=bf16),
-            [VMEM],
+            shape(2 * count, gates),
+            [VMEM] * 2,
             VMEM,
-            [],
+            [yb],
             flops=LONG >> 6,
-        )(others_rest[k - 1])
+        )(others_rest[k - 1], wb)
         token = call(
             meet_kernel, "meet", shape(8, TILE), [any_space] * 2, VMEM, [], flops=LONG
         )(odd_others[k - 1], ready)
@@ -384,11 +385,11 @@
             functools.partial(other_kernel, k),
             "other",
             out_shape,
-            [VMEM] * 6 + [any_space] * 2,
+            [VMEM] * 5 + [any_space] * 2,
             any_space,
             [ya, *dense],
-            input_output_aliases={7: 0},
-        )(ready, even_others[k - 1], odd_others[k - 1], partials[k - 1], wa, wb, token, out)
+            input_output_aliases={6: 0},
+        )(ready, even_others[k - 1], odd_others[k - 1], partials[k - 1], wa, token, out)
     return out.transpose(0, 2, 1, 3).reshape(2, count, pulses, gates)
 
 

time: 19.3 us -> 19.3 us (level)
  transfers between devices with their start and end apart: 7 -> 7, of which waited for: 4 -> 3; matrix products, arithmetic and copies ran while one was open for 6% -> 6% of each run, Pallas kernels for 24% -> 25%
where the time goes in v6:
time: 19.3 us; the launch traced here: 19.1 us
  starting transfers between devices  7.68 us (40%)
  Pallas kernels  6.24 us (32%)
  waiting for transfers between devices  3.34 us (17%)
  local copies, waits for them, and re-layouts  1.77 us (9%)
    ppermute x2, starting transfers between devices, shifted(): lax.ppermute(value, axis, [(i, (i + steps) % count) for i in range(count)])  5 us
    pallas_call x1, Pallas kernels, body(): call(functools.partial(own_kernel, groups, others), 'own', [out_shape] +...  2.78 us
    ppermute x3, starting transfers between devices, from_odd(): return lax.ppermute(value, 'range', list(target.items()))  2.17 us
    ppermute x2, waiting for transfers between devices, shifted(): lax.ppermute(value, axis, [(i, (i + steps) % count) for i in range(count)])  2.03 us
    pallas_call x1, Pallas kernels, body(): call(functools.partial(other_kernel, k), 'other', out_shape, [VMEM] * 5 +...  1.39 us
    ppermute x3, waiting for transfers between devices, from_odd(): return lax.ppermute(value, 'range', list(target.items()))  1.31 us
    slice x1, local copies, waits for them, and re-layouts, body(): raw, rest = (samples[:, :cut], samples[:, cut:])  1.06 us
    pallas_call x1, Pallas kernels, body(): call(prepare_kernel, 'prepare', [shape(span + 1, 2 * TILE, 2 * TILE, dtyp...  1.02 us
  transfers between devices with their start and end apart: 7, of which 3 were waited for; matrix products, arithmetic and copies ran while one was open for 6% of the time, Pallas kernels for 25%

profile of v6, /device:TPU:0, one launch (start us, length us, event | category | flops | bytes accessed | tf_op | source)
XLA Modules:
  0.0 19.1 jit_solution(5121668777050383328)
XLA Ops:
  0.0 0.5 %collective-permute-start = (f32[2,64,8,128]{3,2,1,0:T(8,128)}, f32[2,64,8,128]{3,2,1,0:T(8,128)S(1)}, u32[]{:S(2)}, u32[]{:S(2)}) collective-permute-start(f32[2,64,8,128]{3,2,1,0:T(8,128)} %bitcast.8), channel_id=1, source_target_pairs={{0,2},{2,0},{4,6},{6,4},{8,10},{10,8},{12,14},{14,12},{16,18},{18,... | collective-permute-start | bytes 1572872 | tf_op jit(solution)/shard_map/ppermute | solution.py:44
  0.5 1.1 %fusion = (f32[2,32,8,128]{3,2,1,0:T(8,128)S(1)}, f32[2,32,8,128]{3,2,1,0:T(8,128)S(1)}) fusion(f32[2,64,8,128]{3,2,1,0:T(8,128)} %bitcast.9), kind=kLoop, calls=%fused_computation | loop fusion | bytes 1048576 | tf_op jit(solution)/shard_map/slice | solution.py:304
  1.5 0.1 collective-permute-start.1
  1.6 2.9 %collective-permute-start.4 = (f32[2,32,8,128]{3,2,1,0:T(8,128)S(1)}, f32[2,32,8,128]{3,2,1,0:T(8,128)S(1)}, u32[]{:S(2)}, u32[]{:S(2)}) collective-permute-start(f32[2,32,8,128]{3,2,1,0:T(8,128)S(1)} %get-tuple-element.23.own), channel_id=1, source_target_pairs={{0,1},{1,0},{2,3},{3,2},{4,5},{5,4},{6,7},{7,6},{8,9},{9,8},{10,11... | collective-permute-start | bytes 786440 | tf_op jit(solution)/shard_map/ppermute | solution.py:28
  4.6 0.8 %collective-permute-start.3 = (f32[2,32,8,128]{3,2,1,0:T(8,128)S(1)}, f32[2,32,8,128]{3,2,1,0:T(8,128)S(1)}, u32[]{:S(2)}, u32[]{:S(2)}) collective-permute-start(f32[2,32,8,128]{3,2,1,0:T(8,128)S(1)} %get-tuple-element.23.own), channel_id=1, source_target_pairs={{0,2},{2,4},{4,0},{6,8},{8,10},{10,12},{12,6},{14,16},{16,18},{18,... | collective-permute-start | bytes 786440 | tf_op jit(solution)/shard_map/ppermute | solution.py:39
  5.4 0.0 copy-start.1
  5.4 0.7 %copy-done.1 = f32[2,1024]{1,0:T(2,128)S(1)} copy-done((f32[2,1024]{1,0:T(2,128)S(1)}, f32[2,1024]{1,0:T(2,128)}, u32[]{:S(2)}) %copy-start.1) | copy-done | bytes 8216
  6.1 1.0 %prepare.1 = (bf16[9,256,256]{2,1,0:T(8,128)(2,1)S(1)}, bf16[9,256,256]{2,1,0:T(8,128)(2,1)S(1)}, f32[256,256]{1,0:T(8,128)S(1)}) custom-call(f32[2,1024]{1,0:T(2,128)S(1)} %copy-done.1, f32[2,32,8,128]{3,2,1,0:T(8,128)S(1)} %get-tuple-element.24.rest), custom_call_target="tpu_custom_call" | custom-call | flops 1000 | bytes 1000 | tf_op jit(solution)/shard_map/prepare/pallas_call | solution.py:310
  7.1 1.3 %collective-permute-done.1.odd = f32[2,32,8,128]{3,2,1,0:T(8,128)S(1)} collective-permute-done((f32[2,32,8,128]{3,2,1,0:T(8,128)S(1)}, f32[2,32,8,128]{3,2,1,0:T(8,128)S(1)}, u32[]{:S(2)}, u32[]{:S(2)}) %collective-permute-start.1) | collective-permute-done | bytes 262176 | tf_op jit(solution)/shard_map/ppermute | solution.py:39
  8.4 0.0 collective-permute-done.even
  8.5 2.1 %collective-permute-start.2 = (f32[256,256]{1,0:T(8,128)S(1)}, f32[256,256]{1,0:T(8,128)S(1)}, u32[]{:S(2)}, u32[]{:S(2)}) collective-permute-start(f32[256,256]{1,0:T(8,128)S(1)} %rest.1.after), channel_id=1, source_target_pairs={{0,1},{1,0},{2,3},{3,2},{4,5},{5,4},{6,7},{7,6},{8,9},{9,8},{10,11... | collective-permute-start | bytes 786440 | tf_op jit(solution)/shard_map/ppermute | solution.py:28
  10.5 0.6 %collective-permute-done.4.refs_0_.own = f32[2,32,8,128]{3,2,1,0:T(8,128)S(1)} collective-permute-done((f32[2,32,8,128]{3,2,1,0:T(8,128)S(1)}, f32[2,32,8,128]{3,2,1,0:T(8,128)S(1)}, u32[]{:S(2)}, u32[]{:S(2)}) %collective-permute-start.4) | collective-permute-done | bytes 262176 | tf_op jit(solution)/shard_map/ppermute | solution.py:28
  11.1 0.0 copy-start
  11.1 0.0 copy-start.2
  11.1 1.2 %collective-permute-start.6 = (f32[256,256]{1,0:T(8,128)S(1)}, f32[256,256]{1,0:T(8,128)S(1)}, u32[]{:S(2)}, u32[]{:S(2)}) collective-permute-start(f32[256,256]{1,0:T(8,128)S(1)} %spill.3), channel_id=1, source_target_pairs={{0,2},{2,4},{4,0},{6,8},{8,10},{10,12},{12,6},{14,16},{16,18},{18,... | collective-permute-start | bytes 786440 | tf_op jit(solution)/shard_map/ppermute | solution.py:39
  12.3 0.7 %spill.2 = f32[256,256]{1,0:T(8,128)S(1)} custom-call(f32[2,32,8,128]{3,2,1,0:T(8,128)S(1)} %collective-permute-done.4.refs_0_.own, f32[256,256]{1,0:T(8,128)S(1)} %rest.1.after, bf16[9,256,256]{2,1,0:T(8,128)(2,1)S(1)} %get-tuple-element.15.th, bf16[9,256,256]{2,1,0:T(8,128)(2,1)S(1)} %get-tuple-element.16.tl), custom_call_target="tpu_custom_call" | custom-call | flops 1000 | bytes 1000 | tf_op jit(solution)/shard_map/spill/pallas_call | solution.py:331
  13.0 0.1 collective-permute-start.5
  13.1 0.0 collective-permute-done.3.odd
  13.1 0.0 copy-done
  13.1 0.0 copy-done.2
  13.1 2.8 %own.1 = (f32[256,8,2,128]{3,2,1,0:T(2,128)}, bf16[256,192]{1,0:T(8,128)(2,1)S(1)}, bf16[256,192]{1,0:T(8,128)(2,1)S(1)}, f32[256,256]{1,0:T(8,128)S(1)}) custom-call(s32[4,8]{1,0:T(4,128)S(1)} %bitcast.7, f32[16,2,8,32]{3,2,1,0:T(8,128)S(1)} %bitcast.6, f32[2,64,8,128]{3,2,1,0:T(8,128)S(1)} %collective-permute-done.even, ...), custom_call_target="tpu_custom_call" | custom-call | flops 1000 | bytes 1000 | tf_op jit(solution)/shard_map/own/pallas_call | solution.py:343
  15.9 1.4 %collective-permute-done.2.rest = f32[256,256]{1,0:T(8,128)S(1)} collective-permute-done((f32[256,256]{1,0:T(8,128)S(1)}, f32[256,256]{1,0:T(8,128)S(1)}, u32[]{:S(2)}, u32[]{:S(2)}) %collective-permute-start.2) | collective-permute-done | bytes 262176 | tf_op jit(solution)/shard_map/ppermute | solution.py:28
  17.4 0.3 %ready.1.yb.part = f32[256,1024]{1,0:T(8,128)S(1)} custom-call(f32[256,256]{1,0:T(8,128)S(1)} %collective-permute-done.2.rest, bf16[256,192]{1,0:T(8,128)(2,1)S(1)} %get-tuple-element.19.wb), custom_call_target="tpu_custom_call" | custom-call | flops 1073741824 | bytes 1000 | tf_op jit(solution)/shard_map/ready/pallas_call | solution.py:372
  17.7 0.0 collective-permute-done.6.odd
  17.7 0.0 collective-permute-done.5.even
  17.7 1.4 %other.1 = f32[256,8,2,128]{3,2,1,0:T(2,128)} custom-call(f32[256,1024]{1,0:T(8,128)S(1)} %ready.1.yb.part, f32[256,256]{1,0:T(8,128)S(1)} %collective-permute-done.5.even, f32[256,256]{1,0:T(8,128)S(1)} %collective-permute-done.6.odd, f32[256,256]{1,0:T(8,128)S(1)} %get-tuple-element.20.partial, ...), custom_call_target="tpu_custom_call", output_to_operand_aliasing={{}: (6, {})} | custom-call | flops 1000 | bytes 1000 | tf_op jit(solution)/shard_map/other/pallas_call | solution.py:384
  (3 shorter events, 0.0 us)
Async XLA Ops:
  0.0 8.5 %collective-permute-start = (f32[2,64,8,128]{3,2,1,0:T(8,128)}, f32[2,64,8,128]{3,2,1,0:T(8,128)S(1)}, u32[]{:S(2)}, u32[]{:S(2)}) collective-permute-start(f32[2,64,8,128]{3,2,1,0:T(8,128)} %bitcast.8), channel_id=1, source_target_pairs={{0,2},{2,0},{4,6},{6,4},{8,10},{10,8},{12,14},{14,12},{16,18},{18,... | collective-permute-start | bytes 1572872 | tf_op jit(solution)/shard_map/ppermute | solution.py:44
  1.5 6.9 %collective-permute-start.1 = (f32[2,32,8,128]{3,2,1,0:T(8,128)S(1)}, f32[2,32,8,128]{3,2,1,0:T(8,128)S(1)}, u32[]{:S(2)}, u32[]{:S(2)}) collective-permute-start(f32[2,32,8,128]{3,2,1,0:T(8,128)S(1)} %get-tuple-element.24.rest), channel_id=1, source_target_pairs={{0,2},{2,4},{4,0},{6,8},{8,10},{10,12},{12,6},{14,16},{16,18},{18,... | collective-permute-start | bytes 786440 | tf_op jit(solution)/shard_map/ppermute | solution.py:39
  1.6 9.5 %collective-permute-start.4 = (f32[2,32,8,128]{3,2,1,0:T(8,128)S(1)}, f32[2,32,8,128]{3,2,1,0:T(8,128)S(1)}, u32[]{:S(2)}, u32[]{:S(2)}) collective-permute-start(f32[2,32,8,128]{3,2,1,0:T(8,128)S(1)} %get-tuple-element.23.own), channel_id=1, source_target_pairs={{0,1},{1,0},{2,3},{3,2},{4,5},{5,4},{6,7},{7,6},{8,9},{9,8},{10,11... | collective-permute-start | bytes 786440 | tf_op jit(solution)/shard_map/ppermute | solution.py:28
  4.6 8.5 %collective-permute-start.3 = (f32[2,32,8,128]{3,2,1,0:T(8,128)S(1)}, f32[2,32,8,128]{3,2,1,0:T(8,128)S(1)}, u32[]{:S(2)}, u32[]{:S(2)}) collective-permute-start(f32[2,32,8,128]{3,2,1,0:T(8,128)S(1)} %get-tuple-element.23.own), channel_id=1, source_target_pairs={{0,2},{2,4},{4,0},{6,8},{8,10},{10,12},{12,6},{14,16},{16,18},{18,... | collective-permute-start | bytes 786440 | tf_op jit(solution)/shard_map/ppermute | solution.py:39
  5.4 0.7 %copy-start.1 = (f32[2,1024]{1,0:T(2,128)S(1)}, f32[2,1024]{1,0:T(2,128)}, u32[]{:S(2)}) copy-start(f32[2,1024]{1,0:T(2,128)} %taps.1) | copy-start | bytes 24580
  8.5 8.9 %collective-permute-start.2 = (f32[256,256]{1,0:T(8,128)S(1)}, f32[256,256]{1,0:T(8,128)S(1)}, u32[]{:S(2)}, u32[]{:S(2)}) collective-permute-start(f32[256,256]{1,0:T(8,128)S(1)} %rest.1.after), channel_id=1, source_target_pairs={{0,1},{1,0},{2,3},{3,2},{4,5},{5,4},{6,7},{7,6},{8,9},{9,8},{10,11... | collective-permute-start | bytes 786440 | tf_op jit(solution)/shard_map/ppermute | solution.py:28
  11.1 2.0 %copy-start = (f32[16,2,32,8]{2,3,1,0:T(8,128)S(1)}, f32[16,2,32,8]{2,3,1,0:T(8,128)}, u32[]{:S(2)}) copy-start(f32[16,2,32,8]{2,3,1,0:T(8,128)} %param.5) | copy-start | bytes 98308
  11.1 2.0 %copy-start.2 = (s32[8,4]{0,1:T(4,128)S(1)}, s32[8,4]{0,1:T(4,128)}, u32[]{:S(2)}) copy-start(s32[8,4]{0,1:T(4,128)} %param.6) | copy-start | bytes 388
  11.1 6.6 %collective-permute-start.6 = (f32[256,256]{1,0:T(8,128)S(1)}, f32[256,256]{1,0:T(8,128)S(1)}, u32[]{:S(2)}, u32[]{:S(2)}) collective-permute-start(f32[256,256]{1,0:T(8,128)S(1)} %spill.3), channel_id=1, source_target_pairs={{0,2},{2,4},{4,0},{6,8},{8,10},{10,12},{12,6},{14,16},{16,18},{18,... | collective-permute-start | bytes 786440 | tf_op jit(solution)/shard_map/ppermute | solution.py:39
  13.0 4.7 %collective-permute-start.5 = (f32[256,256]{1,0:T(8,128)S(1)}, f32[256,256]{1,0:T(8,128)S(1)}, u32[]{:S(2)}, u32[]{:S(2)}) collective-permute-start(f32[256,256]{1,0:T(8,128)S(1)} %spill.2), channel_id=1, source_target_pairs={{0,2},{2,0},{4,6},{6,4},{8,10},{10,8},{12,14},{14,12},{16,18},{18,... | collective-permute-start | bytes 786440 | tf_op jit(solution)/shard_map/ppermute | solution.py:44

commit v7 on v4

--- a/solution.py
+++ b/solution.py
@@ -310,6 +310,7 @@
     raw, rest = samples[:, :cut], samples[:, cut:]
     odd_rest = from_odd(rest[:, :, tail])
     others_raw = [shifted(raw, "pulse", k) for k in range(1, pulses)]
+    samples, raw, rest = lax.optimization_barrier((samples, raw, rest))
     even = from_even(samples[:, :, tail])
     odd_raw = from_odd(raw[:, :, tail])
 

time: 19.3 us -> 19.3 us (level)
  waiting for transfers between devices: 3.4 us -> 3.2 us
  transfers between devices with their start and end apart: 7 -> 7, of which waited for: 4 -> 3; matrix products, arithmetic and copies ran while one was open for 6% -> 0% of each run, Pallas kernels for 24% -> 24%
where the time goes in v7:
time: 19.3 us; the launch traced here: 19 us
  starting transfers between devices  7.83 us (41%)
  Pallas kernels  6.06 us (31%)
  waiting for transfers between devices  3.2 us (17%)
  local copies, waits for them, and re-layouts  1.77 us (9%)
    ppermute x2, starting transfers between devices, shifted(): lax.ppermute(value, axis, [(i, (i + steps) % count) for i in range(count)])  4.98 us
    pallas_call x1, Pallas kernels, body(): call(functools.partial(own_kernel, groups, others), 'own', [out_shape] +...  2.78 us
    ppermute x3, starting transfers between devices, from_odd(): return lax.ppermute(value, 'range', list(target.items()))  2.26 us
    ppermute x2, waiting for transfers between devices, shifted(): lax.ppermute(value, axis, [(i, (i + steps) % count) for i in range(count)])  1.88 us
    pallas_call x1, Pallas kernels, body(): call(functools.partial(other_kernel, k), 'other', out_shape, [VMEM] * 6 +...  1.49 us
    ppermute x3, waiting for transfers between devices, from_odd(): return lax.ppermute(value, 'range', list(target.items()))  1.31 us
    slice x1, local copies, waits for them, and re-layouts, body(): raw, rest = (samples[:, :cut], samples[:, cut:])  1.06 us
    pallas_call x1, Pallas kernels, body(): call(prepare_kernel, 'prepare', [shape(span + 1, 2 * TILE, 2 * TILE, dtyp...  1.02 us
  transfers between devices with their start and end apart: 7, of which 3 were waited for; matrix products, arithmetic and copies ran while one was open for 0% of the time, Pallas kernels for 24%

profile of v7, /device:TPU:0, one launch (start us, length us, event | category | flops | bytes accessed | tf_op | source)
XLA Modules:
  0.0 19.0 jit_solution(7545240081981641995)
XLA Ops:
  0.0 1.1 %fusion = (f32[2,32,8,128]{3,2,1,0:T(8,128)S(1)}, f32[2,32,8,128]{3,2,1,0:T(8,128)S(1)}) fusion(f32[2,64,8,128]{3,2,1,0:T(8,128)} %bitcast.8), kind=kLoop, calls=%fused_computation | loop fusion | bytes 1048576 | tf_op jit(solution)/shard_map/slice | solution.py:310
  1.1 0.5 %collective-permute-start = (f32[2,64,8,128]{3,2,1,0:T(8,128)}, f32[2,64,8,128]{3,2,1,0:T(8,128)S(1)}, u32[]{:S(2)}, u32[]{:S(2)}) collective-permute-start(f32[2,64,8,128]{3,2,1,0:T(8,128)} %bitcast.9), channel_id=1, source_target_pairs={{0,2},{2,0},{4,6},{6,4},{8,10},{10,8},{12,14},{14,12},{16,18},{18,... | collective-permute-start | bytes 1572872 | tf_op jit(solution)/shard_map/ppermute | solution.py:44
  1.6 0.1 collective-permute-start.1
  1.7 2.9 %collective-permute-start.3 = (f32[2,32,8,128]{3,2,1,0:T(8,128)S(1)}, f32[2,32,8,128]{3,2,1,0:T(8,128)S(1)}, u32[]{:S(2)}, u32[]{:S(2)}) collective-permute-start(f32[2,32,8,128]{3,2,1,0:T(8,128)S(1)} %get-tuple-element.24.own), channel_id=1, source_target_pairs={{0,1},{1,0},{2,3},{3,2},{4,5},{5,4},{6,7},{7,6},{8,9},{9,8},{10,11... | collective-permute-start | bytes 786440 | tf_op jit(solution)/shard_map/ppermute | solution.py:28
  4.6 0.9 %collective-permute-start.6 = (f32[2,32,8,128]{3,2,1,0:T(8,128)S(1)}, f32[2,32,8,128]{3,2,1,0:T(8,128)S(1)}, u32[]{:S(2)}, u32[]{:S(2)}) collective-permute-start(f32[2,32,8,128]{3,2,1,0:T(8,128)S(1)} %get-tuple-element.24.own), channel_id=1, source_target_pairs={{0,2},{2,4},{4,0},{6,8},{8,10},{10,12},{12,6},{14,16},{16,18},{18,... | collective-permute-start | bytes 786440 | tf_op jit(solution)/shard_map/ppermute | solution.py:39
  5.5 0.0 copy-start.1
  5.5 0.7 %copy-done.1 = f32[2,1024]{1,0:T(2,128)S(1)} copy-done((f32[2,1024]{1,0:T(2,128)S(1)}, f32[2,1024]{1,0:T(2,128)}, u32[]{:S(2)}) %copy-start.1) | copy-done | bytes 8216
  6.2 1.0 %prepare.1 = (bf16[9,256,256]{2,1,0:T(8,128)(2,1)S(1)}, bf16[9,256,256]{2,1,0:T(8,128)(2,1)S(1)}, f32[256,256]{1,0:T(8,128)S(1)}) custom-call(f32[2,1024]{1,0:T(2,128)S(1)} %copy-done.1, f32[2,32,8,128]{3,2,1,0:T(8,128)S(1)} %get-tuple-element.18.rest), custom_call_target="tpu_custom_call" | custom-call | flops 1000 | bytes 1000 | tf_op jit(solution)/shard_map/prepare/pallas_call | solution.py:317
  7.2 1.3 %collective-permute-done.1.odd = f32[2,32,8,128]{3,2,1,0:T(8,128)S(1)} collective-permute-done((f32[2,32,8,128]{3,2,1,0:T(8,128)S(1)}, f32[2,32,8,128]{3,2,1,0:T(8,128)S(1)}, u32[]{:S(2)}, u32[]{:S(2)}) %collective-permute-start.1) | collective-permute-done | bytes 262176 | tf_op jit(solution)/shard_map/ppermute | solution.py:39
  8.5 0.0 collective-permute-done.even
  8.6 2.1 %collective-permute-start.2 = (f32[256,256]{1,0:T(8,128)S(1)}, f32[256,256]{1,0:T(8,128)S(1)}, u32[]{:S(2)}, u32[]{:S(2)}) collective-permute-start(f32[256,256]{1,0:T(8,128)S(1)} %rest.1.after), channel_id=1, source_target_pairs={{0,1},{1,0},{2,3},{3,2},{4,5},{5,4},{6,7},{7,6},{8,9},{9,8},{10,11... | collective-permute-start | bytes 786440 | tf_op jit(solution)/shard_map/ppermute | solution.py:28
  10.6 0.4 %collective-permute-done.3.own.refs_0_ = f32[2,32,8,128]{3,2,1,0:T(8,128)S(1)} collective-permute-done((f32[2,32,8,128]{3,2,1,0:T(8,128)S(1)}, f32[2,32,8,128]{3,2,1,0:T(8,128)S(1)}, u32[]{:S(2)}, u32[]{:S(2)}) %collective-permute-start.3) | collective-permute-done | bytes 262176 | tf_op jit(solution)/shard_map/ppermute | solution.py:28
  11.1 0.0 copy-start
  11.1 0.0 copy-start.2
  11.1 1.3 %collective-permute-start.5 = (f32[256,256]{1,0:T(8,128)S(1)}, f32[256,256]{1,0:T(8,128)S(1)}, u32[]{:S(2)}, u32[]{:S(2)}) collective-permute-start(f32[256,256]{1,0:T(8,128)S(1)} %spill.3), channel_id=1, source_target_pairs={{0,2},{2,4},{4,0},{6,8},{8,10},{10,12},{12,6},{14,16},{16,18},{18,... | collective-permute-start | bytes 786440 | tf_op jit(solution)/shard_map/ppermute | solution.py:39
  12.3 0.7 %spill.2 = f32[256,256]{1,0:T(8,128)S(1)} custom-call(f32[2,32,8,128]{3,2,1,0:T(8,128)S(1)} %collective-permute-done.3.own.refs_0_, f32[256,256]{1,0:T(8,128)S(1)} %rest.1.after, bf16[9,256,256]{2,1,0:T(8,128)(2,1)S(1)} %get-tuple-element.20.th, bf16[9,256,256]{2,1,0:T(8,128)(2,1)S(1)} %get-tuple-element.21.tl), custom_call_target="tpu_custom_call" | custom-call | flops 1000 | bytes 1000 | tf_op jit(solution)/shard_map/spill/pallas_call | solution.py:337
  13.0 0.1 collective-permute-start.4
  13.1 0.0 collective-permute-done.6.odd
  13.1 0.0 copy-done
  13.1 0.0 copy-done.2
  13.1 2.8 %own.1 = (f32[256,8,2,128]{3,2,1,0:T(2,128)}, bf16[256,192]{1,0:T(8,128)(2,1)S(1)}, bf16[256,192]{1,0:T(8,128)(2,1)S(1)}, f32[256,256]{1,0:T(8,128)S(1)}) custom-call(s32[4,8]{1,0:T(4,128)S(1)} %bitcast.7, f32[16,2,8,32]{3,2,1,0:T(8,128)S(1)} %bitcast.6, f32[2,64,8,128]{3,2,1,0:T(8,128)S(1)} %collective-permute-done.even, ...), custom_call_target="tpu_custom_call" | custom-call | flops 1000 | bytes 1000 | tf_op jit(solution)/shard_map/own/pallas_call | solution.py:349
  15.9 1.4 %collective-permute-done.2.rest = f32[256,256]{1,0:T(8,128)S(1)} collective-permute-done((f32[256,256]{1,0:T(8,128)S(1)}, f32[256,256]{1,0:T(8,128)S(1)}, u32[]{:S(2)}, u32[]{:S(2)}) %collective-permute-start.2) | collective-permute-done | bytes 262176 | tf_op jit(solution)/shard_map/ppermute | solution.py:28
  17.4 0.1 ready.1.yb
  17.4 0.0 collective-permute-done.5.odd
  17.5 0.0 collective-permute-done.4.even
  17.5 1.5 %other.1 = f32[256,8,2,128]{3,2,1,0:T(2,128)} custom-call(bf16[192,1024]{1,0:T(8,128)(2,1)S(1)} %ready.1.yb, f32[256,256]{1,0:T(8,128)S(1)} %collective-permute-done.4.even, f32[256,256]{1,0:T(8,128)S(1)} %collective-permute-done.5.odd, f32[256,256]{1,0:T(8,128)S(1)} %get-tuple-element.25.partial, ...), custom_call_target="tpu_custom_call", output_to_operand_aliasing={{}: (7, {})} | custom-call | flops 1000 | bytes 1000 | tf_op jit(solution)/shard_map/other/pallas_call | solution.py:382
  (3 shorter events, 0.0 us)
Async XLA Ops:
  1.1 7.5 %collective-permute-start = (f32[2,64,8,128]{3,2,1,0:T(8,128)}, f32[2,64,8,128]{3,2,1,0:T(8,128)S(1)}, u32[]{:S(2)}, u32[]{:S(2)}) collective-permute-start(f32[2,64,8,128]{3,2,1,0:T(8,128)} %bitcast.9), channel_id=1, source_target_pairs={{0,2},{2,0},{4,6},{6,4},{8,10},{10,8},{12,14},{14,12},{16,18},{18,... | collective-permute-start | bytes 1572872 | tf_op jit(solution)/shard_map/ppermute | solution.py:44
  1.6 6.9 %collective-permute-start.1 = (f32[2,32,8,128]{3,2,1,0:T(8,128)S(1)}, f32[2,32,8,128]{3,2,1,0:T(8,128)S(1)}, u32[]{:S(2)}, u32[]{:S(2)}) collective-permute-start(f32[2,32,8,128]{3,2,1,0:T(8,128)S(1)} %get-tuple-element.18.rest), channel_id=1, source_target_pairs={{0,2},{2,4},{4,0},{6,8},{8,10},{10,12},{12,6},{14,16},{16,18},{18,... | collective-permute-start | bytes 786440 | tf_op jit(solution)/shard_map/ppermute | solution.py:39
  1.7 9.4 %collective-permute-start.3 = (f32[2,32,8,128]{3,2,1,0:T(8,128)S(1)}, f32[2,32,8,128]{3,2,1,0:T(8,128)S(1)}, u32[]{:S(2)}, u32[]{:S(2)}) collective-permute-start(f32[2,32,8,128]{3,2,1,0:T(8,128)S(1)} %get-tuple-element.24.own), channel_id=1, source_target_pairs={{0,1},{1,0},{2,3},{3,2},{4,5},{5,4},{6,7},{7,6},{8,9},{9,8},{10,11... | collective-permute-start | bytes 786440 | tf_op jit(solution)/shard_map/ppermute | solution.py:28
  4.6 8.5 %collective-permute-start.6 = (f32[2,32,8,128]{3,2,1,0:T(8,128)S(1)}, f32[2,32,8,128]{3,2,1,0:T(8,128)S(1)}, u32[]{:S(2)}, u32[]{:S(2)}) collective-permute-start(f32[2,32,8,128]{3,2,1,0:T(8,128)S(1)} %get-tuple-element.24.own), channel_id=1, source_target_pairs={{0,2},{2,4},{4,0},{6,8},{8,10},{10,12},{12,6},{14,16},{16,18},{18,... | collective-permute-start | bytes 786440 | tf_op jit(solution)/shard_map/ppermute | solution.py:39
  5.5 0.7 %copy-start.1 = (f32[2,1024]{1,0:T(2,128)S(1)}, f32[2,1024]{1,0:T(2,128)}, u32[]{:S(2)}) copy-start(f32[2,1024]{1,0:T(2,128)} %taps.1) | copy-start | bytes 24580
  8.6 8.8 %collective-permute-start.2 = (f32[256,256]{1,0:T(8,128)S(1)}, f32[256,256]{1,0:T(8,128)S(1)}, u32[]{:S(2)}, u32[]{:S(2)}) collective-permute-start(f32[256,256]{1,0:T(8,128)S(1)} %rest.1.after), channel_id=1, source_target_pairs={{0,1},{1,0},{2,3},{3,2},{4,5},{5,4},{6,7},{7,6},{8,9},{9,8},{10,11... | collective-permute-start | bytes 786440 | tf_op jit(solution)/shard_map/ppermute | solution.py:28
  11.1 2.1 %copy-start = (f32[16,2,32,8]{2,3,1,0:T(8,128)S(1)}, f32[16,2,32,8]{2,3,1,0:T(8,128)}, u32[]{:S(2)}) copy-start(f32[16,2,32,8]{2,3,1,0:T(8,128)} %param.5) | copy-start | bytes 98308
  11.1 2.1 %copy-start.2 = (s32[8,4]{0,1:T(4,128)S(1)}, s32[8,4]{0,1:T(4,128)}, u32[]{:S(2)}) copy-start(s32[8,4]{0,1:T(4,128)} %param.6) | copy-start | bytes 388
  11.1 6.4 %collective-permute-start.5 = (f32[256,256]{1,0:T(8,128)S(1)}, f32[256,256]{1,0:T(8,128)S(1)}, u32[]{:S(2)}, u32[]{:S(2)}) collective-permute-start(f32[256,256]{1,0:T(8,128)S(1)} %spill.3), channel_id=1, source_target_pairs={{0,2},{2,4},{4,0},{6,8},{8,10},{10,12},{12,6},{14,16},{16,18},{18,... | collective-permute-start | bytes 786440 | tf_op jit(solution)/shard_map/ppermute | solution.py:39
  13.0 4.4 %collective-permute-start.4 = (f32[256,256]{1,0:T(8,128)S(1)}, f32[256,256]{1,0:T(8,128)S(1)}, u32[]{:S(2)}, u32[]{:S(2)}) collective-permute-start(f32[256,256]{1,0:T(8,128)S(1)} %spill.2), channel_id=1, source_target_pairs={{0,2},{2,0},{4,6},{6,4},{8,10},{10,8},{12,14},{14,12},{16,18},{18,... | collective-permute-start | bytes 786440 | tf_op jit(solution)/shard_map/ppermute | solution.py:44
